TPU v7x, 32 devices: a whole 2x2x4 slice. The times are simulated.
32 devices in a mesh: segment: 4 (over y, x), blk: 8 (over z, core).
Axes of the slice: x: 2, y: 2, z: 4, core: 2. Of those that a mesh axis runs over, the one named last changes fastest.
Arguments:
- inputs: bfloat16 [4, 128, 64, 128], P(None, 'blk'), may hold values from -6 to 6
- weights: bfloat16 [8, 128, 64, 2048], P('segment', 'blk'), may hold values from -0.1875 to 0.1875
- biases: float32 [8, 128, 64], P('segment', 'blk'), may hold values from -3 to 3
- tile_index: int32 [8, 128, 32], P('segment', 'blk'), may hold values from 0 to 31, each once within a row
Outputs:
- final_activity: bfloat16 [4, 128, 64, 128], P('segment', 'blk')
Inputs may be any that keep to these rules, and one draw needn't show every extreme that they name: `tile_index`: each row of 32 entries names every member 0..31 once.
All inputs are finite; a program needn't handle non-finite values.
Results may differ from a plain program's by a relative error of at most 0.014.
Values may be sent and summed in bfloat16 or wider, within the bound.
No kernel may reach another device: no remote copies, remote signals or barrier semaphores. Data moves between devices by JAX's collectives and lax.ppermute only.
A program may use at most 128 MiB of HBM per device.

v0:
```python
import functools

import jax
import jax.numpy as jnp
from jax import lax
from jax.experimental import pallas as pl
from jax.experimental.pallas import tpu as pltpu
from jax.sharding import PartitionSpec as P

MIB = 1024 * 1024
PLACE_VMEM = 46 * MIB
LAYER_VMEM = 16 * MIB
WEIGHT_COPIES = 4
WHOLE = pl.BlockSpec(memory_space=pltpu.VMEM)
TABLE = pl.BlockSpec(memory_space=pltpu.SMEM)


def place_kernel(layer, order, tile_ref, column_ref, slot_ref, weights_ref, placed_ref, held, arrived):
    slots, tile, width = held.shape
    lanes = 2 * tile
    copies = arrived.shape[0]
    per_copy = slots // copies
    pairs = slots // 2 // copies

    def copy(part):
        these = pl.ds(part * per_copy, per_copy)
        return pltpu.make_async_copy(weights_ref.at[layer, these], held.at[these], arrived.at[part])

    def place(pair):
        both_slots = [slot_ref[2 * pair], slot_ref[2 * pair + 1]]
        for block in range(width // lanes):
            columns = pl.ds(block * lanes, lanes)
            turned = jnp.concatenate([held[slot, :, columns] for slot in both_slots], axis=0).T
            for half in range(2):
                for side, slot in enumerate(both_slots):
                    row = pl.multiple_of(column_ref[layer, tile_ref[layer, slot, 2 * block + half]] * tile, tile)
                    placed_ref[pair, pl.ds(row, tile), pl.ds(side * tile, tile)] = turned[
                        half * tile : (half + 1) * tile, side * tile : (side + 1) * tile
                    ]

    for part in range(copies):
        copy(part).start()
    for part in range(copies):
        copy(part).wait()
        for pair in order[part * pairs : (part + 1) * pairs]:
            place(pair)


def placed_weights(layer, weights, tile_index, columns, slots_of, order):
    _, slots, tile, width = weights.shape
    copies = min(WEIGHT_COPIES, slots // 2)
    return pl.pallas_call(
        functools.partial(place_kernel, layer, order),
        in_specs=[TABLE, TABLE, TABLE, pl.BlockSpec(memory_space=pltpu.HBM)],
        out_specs=WHOLE,
        out_shape=jax.ShapeDtypeStruct((slots // 2, width, 2 * tile), weights.dtype),
        scratch_shapes=[pltpu.VMEM((slots, tile, width), weights.dtype), pltpu.SemaphoreType.DMA((copies,))],
        compiler_params=pltpu.CompilerParams(vmem_limit_bytes=PLACE_VMEM),
        name="place_tiles",
    )(tile_index, columns, slots_of, weights)


def turn_kernel(blocks_ref, turned_ref):
    for index in range(blocks_ref.shape[0]):
        turned_ref[index] = blocks_ref[index].T


def turned(blocks):
    count, rows, columns = blocks.shape
    return pl.pallas_call(
        turn_kernel,
        in_specs=[WHOLE],
        out_specs=WHOLE,
        out_shape=jax.ShapeDtypeStruct((count, columns, rows), blocks.dtype),
        compiler_params=pltpu.CompilerParams(vmem_limit_bytes=LAYER_VMEM),
        name="turn",
    )(blocks)


def layer_kernel(pieces, parts, forwarders, *refs):
    piece_refs, (matrix_ref, offset_ref), refs = refs[:pieces], refs[pieces : pieces + 2], refs[pieces + 2 :]
    kept_refs, out_refs = refs[:-parts], refs[-parts:]
    pairs, _, lanes = matrix_ref.shape
    per_out = pairs // parts
    step = 2 if per_out % 2 == 0 else 1

    def compute():
        values = jnp.concatenate([piece[...] for piece in piece_refs], axis=1)
        for first in range(0, pairs, step):
            matrix = jnp.concatenate([matrix_ref[first + index] for index in range(step)], axis=1)
            total = jnp.dot(values, matrix, preferred_element_type=jnp.float32)
            total = total + offset_ref[:, pl.ds(first * lanes, step * lanes)]
            out_ref = out_refs[first // per_out]
            out_ref[:, pl.ds(first % per_out * lanes, step * lanes)] = jnp.maximum(total, 0.0).astype(out_ref.dtype)

    if not kept_refs:
        compute()
        return
    place_ref, *kept_refs = kept_refs

    @pl.when(place_ref[0] >= forwarders)
    def _():
        compute()

    @pl.when(place_ref[0] < forwarders)
    def _():
        for kept_ref, out_ref in zip(kept_refs, out_refs):
            out_ref[...] = kept_ref[...]


def layer(pieces, matrix, offset, parts, place, forwarders=0, kept=()):
    pairs, width, lanes = matrix.shape
    batch = pieces[0].shape[0]
    outs = parts if pairs % parts == 0 else 1
    extra, kept = ([place], list(kept)) if forwarders else ([], [])
    if outs < parts:
        pieces = [jnp.concatenate(pieces, axis=1)]
        kept = [jnp.concatenate(kept, axis=1)] if kept else []
    result = pl.pallas_call(
        functools.partial(layer_kernel, len(pieces), outs, forwarders),
        in_specs=[WHOLE] * (len(pieces) + 2) + [TABLE] * len(extra) + [WHOLE] * len(kept),
        out_specs=[WHOLE] * outs,
        out_shape=[jax.ShapeDtypeStruct((batch, pairs * lanes // outs), pieces[0].dtype)] * outs,
        cost_estimate=pl.CostEstimate(
            flops=2 * batch * width * pairs * lanes, bytes_accessed=2 * pairs * width * lanes, transcendentals=0
        ),
        compiler_params=pltpu.CompilerParams(vmem_limit_bytes=LAYER_VMEM),
        name="layer",
    )(*pieces, matrix, offset, *extra, *kept)
    return list(result) if outs == parts else jnp.split(result[0], parts, axis=1)


def finish_kernel(place_ref, *refs):
    out_ref = refs[-1]
    deep, group, tile, batch = out_ref.shape
    part_refs, exchanged_refs = refs[:group], refs[group:-1]
    odd = place_ref[0] % 2 == 1
    for x in range(group):
        value = part_refs[x][...]
        if x:
            value = jnp.where(odd, exchanged_refs[x - 1][...], value)
        out_ref[:, place_ref[1] ^ x] = value.T.reshape(deep, tile, batch)


def finished(parts, exchanged, place, shape):
    return pl.pallas_call(
        finish_kernel,
        in_specs=[TABLE] + [WHOLE] * (len(parts) + len(exchanged)),
        out_specs=WHOLE,
        out_shape=jax.ShapeDtypeStruct(shape, parts[0].dtype),
        compiler_params=pltpu.CompilerParams(vmem_limit_bytes=LAYER_VMEM),
        name="finish",
    )(place, *parts, *exchanged)


def body(inputs, weights, biases, tile_index):
    micro_count, local, tile, batch = inputs.shape
    fan = tile_index.shape[2]
    segments, devices = lax.axis_size("segment"), lax.axis_size("blk")
    assert micro_count == segments and segments % 2 == 0
    group = min(local, devices // 4)
    deep = local // group
    part_width = deep * tile
    segment, position = lax.axis_index("segment"), lax.axis_index("blk")
    core, near, far = position & 1, (position >> 1) & (group - 1), position // (2 * group) & 1

    member = jnp.arange(fan, dtype=jnp.int32)
    member_digit, member_slot = member // local, member % local
    in_part = ((member_slot % group) ^ near) * deep + member_slot // group
    even_columns = (member_digit ^ core) * local + jnp.where(segment == 0, member_slot, in_part)
    odd_columns = (member_digit ^ far) * local + in_part
    columns = jnp.stack([even_columns, odd_columns])
    spot = jnp.arange(local, dtype=jnp.int32)
    slots_of = spot % deep * group + ((spot // deep) ^ near)
    first_of = [(2 * pair) % deep * group if deep > 1 else 2 * pair for pair in range(local // 2)]
    order = sorted(range(local // 2), key=lambda pair: (first_of[pair], pair))
    offsets = biases.reshape(biases.shape[0], deep, group, tile)
    offsets = jnp.stack([lax.dynamic_index_in_dim(offsets, near ^ x, 2, keepdims=False) for x in range(group)], axis=1)
    offsets = offsets.reshape(biases.shape[0], 1, local * tile)
    place = jnp.stack([segment, near]).astype(jnp.int32)
    columns, slots_of, place, first, offsets = lax.optimization_barrier((columns, slots_of, place, segment == 0, offsets))
    matrices = [placed_weights(index, weights, tile_index, columns, slots_of, order) for index in range(2)]

    def along(value, flip):
        return lax.ppermute(value, "blk", [(i, i ^ flip) for i in range(devices)])

    def exchange(parts):
        pieces = {0: parts[0]}
        for x in [*range(group, 2 * group), *range(1, group)]:
            pieces[x] = along(parts[x % group], 2 * x)
        return [pieces[x] for x in range(2 * group)]

    def passed(parts):
        return [
            lax.ppermute(
                part,
                ("segment", "blk"),
                [(s * devices + i, (s + 1) % segments * devices + (i ^ 2 * x)) for s in range(segments) for i in range(devices)],
            )
            for x, part in enumerate(parts)
        ]

    sequence = [*range(segments - 2, -1, -1), segments - 1]
    turns = micro_count + segments - 1
    arriving = ()
    for turn in range(turns):
        if turn == 0:
            new = inputs[sequence[turn]].reshape(local * tile, batch)
            pieces = list(turned(jnp.stack([new, along(new, 1)])))
        elif turn < micro_count:
            new = turned(inputs[sequence[turn]].reshape(1, local * tile, batch))[0]
            new = [new[:, x * part_width : (x + 1) * part_width] for x in range(group)]
            pieces = [jnp.where(first, a, b) for a, b in zip(new, arriving)]
        else:
            pieces = arriving
        if turn:
            pieces = pieces + [along(part, 1) for part in pieces]
        parts = layer(pieces, matrices[0], offsets[0], group, place)
        pieces = exchange(parts)
        forwarders = max(0, turn - micro_count + 1)
        parts = layer(pieces, matrices[1], offsets[1], group, place, forwarders, arriving)
        if turn < turns - 1:
            arriving = passed(parts)

    exchanged = [along(parts[x], 2 * x) for x in range(1, group)]
    return finished(parts, exchanged, place, (deep, group, tile, batch)).reshape(1, local, tile, batch)


def solution(mesh):
    in_specs = (
        P(None, "blk", None, None),
        P("segment", "blk", None, None),
        P("segment", "blk", None),
        P("segment", "blk", None),
    )
    out_specs = P("segment", "blk", None, None)
    return jax.shard_map(body, mesh=mesh, in_specs=in_specs, out_specs=out_specs, check_vma=False)
```

profile of v0, /device:TPU:0, one launch (start us, length us, event | category | flops | bytes accessed | tf_op | source)
XLA Modules:
  0.0 185.6 jit_solution(9863530723933065158)
XLA Ops:
  3.5 3.9 %place_tiles.2.refs_2_.refs_4_ = bf16[8,2048,128]{2,1,0:T(8,128)(2,1)S(1)} custom-call(s32[2,16,32]{2,1,0:T(8,128)S(1)} %copy-done, s32[2,32]{1,0:T(2,128)S(1)} %pad_add_fusion.column_ref, s32[16]{0:T(128)S(1)} %fusion.5.slot_ref, bf16[2,16,64,2048]{3,2,1,0:T(8,128)(2,1)} %weights_ref.3), custom_call_target="tpu_custom_call" | custom-call | tf_op jit(solution)/shard_map/place_tiles/pallas_call | solution.py:52
  8.5 3.7 %collective-permute-start.2 = (bf16[128,512]{1,0:T(8,128)(2,1)S(1)}, bf16[128,512]{1,0:T(8,128)(2,1)S(1)}, u32[]{:S(2)}, u32[]{:S(2)}) collective-permute-start(bf16[128,512]{1,0:T(8,128)(2,1)S(1)} %get-tuple-element.43.refs_0_), channel_id=1, source_target_pairs={{0,4},{1,5},{2,6},{3,7},{4,0},{5,1},{6,2},{7,3},{8,12},{9,13},{10,... | collective-permute-start | bytes 393224 | tf_op jit(solution)/shard_map/ppermute | solution.py:185
  13.8 4.3 %place_tiles.3.refs_4_ = bf16[8,2048,128]{2,1,0:T(8,128)(2,1)S(1)} custom-call(s32[2,16,32]{2,1,0:T(8,128)S(1)} %copy-done, s32[2,32]{1,0:T(2,128)S(1)} %pad_add_fusion.column_ref, s32[16]{0:T(128)S(1)} %fusion.5.slot_ref, bf16[2,16,64,2048]{3,2,1,0:T(8,128)(2,1)} %weights_ref.3), custom_call_target="tpu_custom_call" | custom-call | tf_op jit(solution)/shard_map/place_tiles/pallas_call | solution.py:52
  18.1 4.1 %collective-permute-done.2.refs_2_ = bf16[128,512]{1,0:T(8,128)(2,1)S(1)} collective-permute-done((bf16[128,512]{1,0:T(8,128)(2,1)S(1)}, bf16[128,512]{1,0:T(8,128)(2,1)S(1)}, u32[]{:S(2)}, u32[]{:S(2)}) %collective-permute-start.2) | collective-permute-done | bytes 131104 | tf_op jit(solution)/shard_map/ppermute | solution.py:185
  25.6 3.1 %collective-permute-start.5 = (bf16[128,512]{1,0:T(8,128)(2,1)S(1)}, bf16[128,512]{1,0:T(8,128)(2,1)S(1)}, u32[]{:S(2)}, u32[]{:S(2)}) collective-permute-start(bf16[128,512]{1,0:T(8,128)(2,1)S(1)} %get-tuple-element.46), channel_id=1, source_target_pairs={{0,10},{1,11},{2,8},{3,9},{4,14},{5,15},{6,12},{7,13},{8,18},{9,19... | collective-permute-start | bytes 393224 | tf_op jit(solution)/shard_map/ppermute | solution.py:195
  28.9 3.9 %collective-permute-done.4 = bf16[128,512]{1,0:T(8,128)(2,1)S(1)} collective-permute-done((bf16[128,512]{1,0:T(8,128)(2,1)S(1)}, bf16[128,512]{1,0:T(8,128)(2,1)S(1)}, u32[]{:S(2)}, u32[]{:S(2)}) %collective-permute-start.4) | collective-permute-done | bytes 131104 | tf_op jit(solution)/shard_map/ppermute | solution.py:195
  35.1 4.7 %collective-permute-start.9 = (bf16[128,512]{1,0:T(8,128)(2,1)S(1)}, bf16[128,512]{1,0:T(8,128)(2,1)S(1)}, u32[]{:S(2)}, u32[]{:S(2)}) collective-permute-start(bf16[128,512]{1,0:T(8,128)(2,1)S(1)} %get-tuple-element.47.refs_0_), channel_id=1, source_target_pairs={{0,4},{1,5},{2,6},{3,7},{4,0},{5,1},{6,2},{7,3},{8,12},{9,13},{10,... | collective-permute-start | bytes 393224 | tf_op jit(solution)/shard_map/ppermute | solution.py:185
  40.5 9.3 %collective-permute-done.9.refs_2_ = bf16[128,512]{1,0:T(8,128)(2,1)S(1)} collective-permute-done((bf16[128,512]{1,0:T(8,128)(2,1)S(1)}, bf16[128,512]{1,0:T(8,128)(2,1)S(1)}, u32[]{:S(2)}, u32[]{:S(2)}) %collective-permute-start.9) | collective-permute-done | bytes 131104 | tf_op jit(solution)/shard_map/ppermute | solution.py:185
  52.2 3.9 %collective-permute-start.12 = (bf16[128,512]{1,0:T(8,128)(2,1)S(1)}, bf16[128,512]{1,0:T(8,128)(2,1)S(1)}, u32[]{:S(2)}, u32[]{:S(2)}) collective-permute-start(bf16[128,512]{1,0:T(8,128)(2,1)S(1)} %get-tuple-element.50), channel_id=1, source_target_pairs={{0,10},{1,11},{2,8},{3,9},{4,14},{5,15},{6,12},{7,13},{8,18},{9,19... | collective-permute-start | bytes 393224 | tf_op jit(solution)/shard_map/ppermute | solution.py:195
  56.2 4.1 %collective-permute-done.11 = bf16[128,512]{1,0:T(8,128)(2,1)S(1)} collective-permute-done((bf16[128,512]{1,0:T(8,128)(2,1)S(1)}, bf16[128,512]{1,0:T(8,128)(2,1)S(1)}, u32[]{:S(2)}, u32[]{:S(2)}) %collective-permute-start.11) | collective-permute-done | bytes 131104 | tf_op jit(solution)/shard_map/ppermute | solution.py:195
  62.7 2.2 %collective-permute-start.16 = (bf16[128,512]{1,0:T(8,128)(2,1)S(1)}, bf16[128,512]{1,0:T(8,128)(2,1)S(1)}, u32[]{:S(2)}, u32[]{:S(2)}) collective-permute-start(bf16[128,512]{1,0:T(8,128)(2,1)S(1)} %get-tuple-element.51.refs_0_), channel_id=1, source_target_pairs={{0,4},{1,5},{2,6},{3,7},{4,0},{5,1},{6,2},{7,3},{8,12},{9,13},{10,... | collective-permute-start | bytes 393224 | tf_op jit(solution)/shard_map/ppermute | solution.py:185
  64.8 2.6 %collective-permute-start.17 = (bf16[128,512]{1,0:T(8,128)(2,1)S(1)}, bf16[128,512]{1,0:T(8,128)(2,1)S(1)}, u32[]{:S(2)}, u32[]{:S(2)}) collective-permute-start(bf16[128,512]{1,0:T(8,128)(2,1)S(1)} %get-tuple-element.52), channel_id=1, source_target_pairs={{0,6},{1,7},{2,4},{3,5},{4,2},{5,3},{6,0},{7,1},{8,14},{9,15},{10,... | collective-permute-start | bytes 393224 | tf_op jit(solution)/shard_map/ppermute | solution.py:185
  67.4 8.2 %collective-permute-done.16.refs_2_ = bf16[128,512]{1,0:T(8,128)(2,1)S(1)} collective-permute-done((bf16[128,512]{1,0:T(8,128)(2,1)S(1)}, bf16[128,512]{1,0:T(8,128)(2,1)S(1)}, u32[]{:S(2)}, u32[]{:S(2)}) %collective-permute-start.16) | collective-permute-done | bytes 131104 | tf_op jit(solution)/shard_map/ppermute | solution.py:185
  77.3 4.3 %collective-permute-start.19 = (bf16[128,512]{1,0:T(8,128)(2,1)S(1)}, bf16[128,512]{1,0:T(8,128)(2,1)S(1)}, u32[]{:S(2)}, u32[]{:S(2)}) collective-permute-start(bf16[128,512]{1,0:T(8,128)(2,1)S(1)} %get-tuple-element.54), channel_id=1, source_target_pairs={{0,10},{1,11},{2,8},{3,9},{4,14},{5,15},{6,12},{7,13},{8,18},{9,19... | collective-permute-start | bytes 393224 | tf_op jit(solution)/shard_map/ppermute | solution.py:195
  81.7 4.1 %collective-permute-done.18 = bf16[128,512]{1,0:T(8,128)(2,1)S(1)} collective-permute-done((bf16[128,512]{1,0:T(8,128)(2,1)S(1)}, bf16[128,512]{1,0:T(8,128)(2,1)S(1)}, u32[]{:S(2)}, u32[]{:S(2)}) %collective-permute-start.18) | collective-permute-done | bytes 131104 | tf_op jit(solution)/shard_map/ppermute | solution.py:195
  88.2 3.0 %collective-permute-start.23 = (bf16[128,512]{1,0:T(8,128)(2,1)S(1)}, bf16[128,512]{1,0:T(8,128)(2,1)S(1)}, u32[]{:S(2)}, u32[]{:S(2)}) collective-permute-start(bf16[128,512]{1,0:T(8,128)(2,1)S(1)} %get-tuple-element.55.refs_0_), channel_id=1, source_target_pairs={{0,4},{1,5},{2,6},{3,7},{4,0},{5,1},{6,2},{7,3},{8,12},{9,13},{10,... | collective-permute-start | bytes 393224 | tf_op jit(solution)/shard_map/ppermute | solution.py:185
  92.6 8.5 %collective-permute-done.23.refs_2_ = bf16[128,512]{1,0:T(8,128)(2,1)S(1)} collective-permute-done((bf16[128,512]{1,0:T(8,128)(2,1)S(1)}, bf16[128,512]{1,0:T(8,128)(2,1)S(1)}, u32[]{:S(2)}, u32[]{:S(2)}) %collective-permute-start.23) | collective-permute-done | bytes 131104 | tf_op jit(solution)/shard_map/ppermute | solution.py:185
  102.9 4.5 %collective-permute-start.26 = (bf16[128,512]{1,0:T(8,128)(2,1)S(1)}, bf16[128,512]{1,0:T(8,128)(2,1)S(1)}, u32[]{:S(2)}, u32[]{:S(2)}) collective-permute-start(bf16[128,512]{1,0:T(8,128)(2,1)S(1)} %get-tuple-element.58), channel_id=1, source_target_pairs={{0,10},{1,11},{2,8},{3,9},{4,14},{5,15},{6,12},{7,13},{8,18},{9,19... | collective-permute-start | bytes 393224 | tf_op jit(solution)/shard_map/ppermute | solution.py:195
  107.4 4.2 %collective-permute-done.25.refs_0_.refs_7_ = bf16[128,512]{1,0:T(8,128)(2,1)S(1)} collective-permute-done((bf16[128,512]{1,0:T(8,128)(2,1)S(1)}, bf16[128,512]{1,0:T(8,128)(2,1)S(1)}, u32[]{:S(2)}, u32[]{:S(2)}) %collective-permute-start.25) | collective-permute-done | bytes 131104 | tf_op jit(solution)/shard_map/ppermute | solution.py:195
  113.9 2.4 %collective-permute-start.30 = (bf16[128,512]{1,0:T(8,128)(2,1)S(1)}, bf16[128,512]{1,0:T(8,128)(2,1)S(1)}, u32[]{:S(2)}, u32[]{:S(2)}) collective-permute-start(bf16[128,512]{1,0:T(8,128)(2,1)S(1)} %get-tuple-element.59.refs_0_), channel_id=1, source_target_pairs={{0,4},{1,5},{2,6},{3,7},{4,0},{5,1},{6,2},{7,3},{8,12},{9,13},{10,... | collective-permute-start | bytes 393224 | tf_op jit(solution)/shard_map/ppermute | solution.py:185
  116.3 2.4 %collective-permute-start.31 = (bf16[128,512]{1,0:T(8,128)(2,1)S(1)}, bf16[128,512]{1,0:T(8,128)(2,1)S(1)}, u32[]{:S(2)}, u32[]{:S(2)}) collective-permute-start(bf16[128,512]{1,0:T(8,128)(2,1)S(1)} %get-tuple-element.60), channel_id=1, source_target_pairs={{0,6},{1,7},{2,4},{3,5},{4,2},{5,3},{6,0},{7,1},{8,14},{9,15},{10,... | collective-permute-start | bytes 393224 | tf_op jit(solution)/shard_map/ppermute | solution.py:185
  118.7 8.2 %collective-permute-done.30.refs_2_ = bf16[128,512]{1,0:T(8,128)(2,1)S(1)} collective-permute-done((bf16[128,512]{1,0:T(8,128)(2,1)S(1)}, bf16[128,512]{1,0:T(8,128)(2,1)S(1)}, u32[]{:S(2)}, u32[]{:S(2)}) %collective-permute-start.30) | collective-permute-done | bytes 131104 | tf_op jit(solution)/shard_map/ppermute | solution.py:185
  128.7 4.7 %collective-permute-start.33 = (bf16[128,512]{1,0:T(8,128)(2,1)S(1)}, bf16[128,512]{1,0:T(8,128)(2,1)S(1)}, u32[]{:S(2)}, u32[]{:S(2)}) collective-permute-start(bf16[128,512]{1,0:T(8,128)(2,1)S(1)} %get-tuple-element.62), channel_id=1, source_target_pairs={{0,10},{1,11},{2,8},{3,9},{4,14},{5,15},{6,12},{7,13},{8,18},{9,19... | collective-permute-start | bytes 393224 | tf_op jit(solution)/shard_map/ppermute | solution.py:195
  133.4 3.5 %collective-permute-done.32.refs_0_.refs_7_ = bf16[128,512]{1,0:T(8,128)(2,1)S(1)} collective-permute-done((bf16[128,512]{1,0:T(8,128)(2,1)S(1)}, bf16[128,512]{1,0:T(8,128)(2,1)S(1)}, u32[]{:S(2)}, u32[]{:S(2)}) %collective-permute-start.32) | collective-permute-done | bytes 131104 | tf_op jit(solution)/shard_map/ppermute | solution.py:195
  139.1 3.0 %collective-permute-start.37 = (bf16[128,512]{1,0:T(8,128)(2,1)S(1)}, bf16[128,512]{1,0:T(8,128)(2,1)S(1)}, u32[]{:S(2)}, u32[]{:S(2)}) collective-permute-start(bf16[128,512]{1,0:T(8,128)(2,1)S(1)} %get-tuple-element.63.refs_0_), channel_id=1, source_target_pairs={{0,4},{1,5},{2,6},{3,7},{4,0},{5,1},{6,2},{7,3},{8,12},{9,13},{10,... | collective-permute-start | bytes 393224 | tf_op jit(solution)/shard_map/ppermute | solution.py:185
  143.6 8.5 %collective-permute-done.37.refs_2_ = bf16[128,512]{1,0:T(8,128)(2,1)S(1)} collective-permute-done((bf16[128,512]{1,0:T(8,128)(2,1)S(1)}, bf16[128,512]{1,0:T(8,128)(2,1)S(1)}, u32[]{:S(2)}, u32[]{:S(2)}) %collective-permute-start.37) | collective-permute-done | bytes 131104 | tf_op jit(solution)/shard_map/ppermute | solution.py:185
  154.1 5.6 %collective-permute-start.40 = (bf16[128,512]{1,0:T(8,128)(2,1)S(1)}, bf16[128,512]{1,0:T(8,128)(2,1)S(1)}, u32[]{:S(2)}, u32[]{:S(2)}) collective-permute-start(bf16[128,512]{1,0:T(8,128)(2,1)S(1)} %get-tuple-element.66), channel_id=1, source_target_pairs={{0,10},{1,11},{2,8},{3,9},{4,14},{5,15},{6,12},{7,13},{8,18},{9,19... | collective-permute-start | bytes 393224 | tf_op jit(solution)/shard_map/ppermute | solution.py:195
  159.6 2.8 %collective-permute-done.39.refs_0_.refs_7_ = bf16[128,512]{1,0:T(8,128)(2,1)S(1)} collective-permute-done((bf16[128,512]{1,0:T(8,128)(2,1)S(1)}, bf16[128,512]{1,0:T(8,128)(2,1)S(1)}, u32[]{:S(2)}, u32[]{:S(2)}) %collective-permute-start.39) | collective-permute-done | bytes 131104 | tf_op jit(solution)/shard_map/ppermute | solution.py:195
  164.7 2.4 %collective-permute-start.44 = (bf16[128,512]{1,0:T(8,128)(2,1)S(1)}, bf16[128,512]{1,0:T(8,128)(2,1)S(1)}, u32[]{:S(2)}, u32[]{:S(2)}) collective-permute-start(bf16[128,512]{1,0:T(8,128)(2,1)S(1)} %get-tuple-element.67.refs_0_), channel_id=1, source_target_pairs={{0,4},{1,5},{2,6},{3,7},{4,0},{5,1},{6,2},{7,3},{8,12},{9,13},{10,... | collective-permute-start | bytes 393224 | tf_op jit(solution)/shard_map/ppermute | solution.py:185
  167.1 2.4 %collective-permute-start.45 = (bf16[128,512]{1,0:T(8,128)(2,1)S(1)}, bf16[128,512]{1,0:T(8,128)(2,1)S(1)}, u32[]{:S(2)}, u32[]{:S(2)}) collective-permute-start(bf16[128,512]{1,0:T(8,128)(2,1)S(1)} %get-tuple-element.68), channel_id=1, source_target_pairs={{0,6},{1,7},{2,4},{3,5},{4,2},{5,3},{6,0},{7,1},{8,14},{9,15},{10,... | collective-permute-start | bytes 393224 | tf_op jit(solution)/shard_map/ppermute | solution.py:185
  169.5 8.2 %collective-permute-done.44.refs_2_ = bf16[128,512]{1,0:T(8,128)(2,1)S(1)} collective-permute-done((bf16[128,512]{1,0:T(8,128)(2,1)S(1)}, bf16[128,512]{1,0:T(8,128)(2,1)S(1)}, u32[]{:S(2)}, u32[]{:S(2)}) %collective-permute-start.44) | collective-permute-done | bytes 131104 | tf_op jit(solution)/shard_map/ppermute | solution.py:185
  181.1 3.2 %collective-permute-done.46.refs_2_ = bf16[128,512]{1,0:T(8,128)(2,1)S(1)} collective-permute-done((bf16[128,512]{1,0:T(8,128)(2,1)S(1)}, bf16[128,512]{1,0:T(8,128)(2,1)S(1)}, u32[]{:S(2)}, u32[]{:S(2)}) %collective-permute-start.46) | collective-permute-done | bytes 131104 | tf_op jit(solution)/shard_map/ppermute | solution.py:185
  (99 shorter events, 41.8 us)
Async XLA Ops:
  8.5 13.7 %collective-permute-start.2 = (bf16[128,512]{1,0:T(8,128)(2,1)S(1)}, bf16[128,512]{1,0:T(8,128)(2,1)S(1)}, u32[]{:S(2)}, u32[]{:S(2)}) collective-permute-start(bf16[128,512]{1,0:T(8,128)(2,1)S(1)} %get-tuple-element.43.refs_0_), channel_id=1, source_target_pairs={{0,4},{1,5},{2,6},{3,7},{4,0},{5,1},{6,2},{7,3},{8,12},{9,13},{10,... | collective-permute-start | bytes 393224 | tf_op jit(solution)/shard_map/ppermute | solution.py:185
  12.2 10.0 %collective-permute-start.3 = (bf16[128,512]{1,0:T(8,128)(2,1)S(1)}, bf16[128,512]{1,0:T(8,128)(2,1)S(1)}, u32[]{:S(2)}, u32[]{:S(2)}) collective-permute-start(bf16[128,512]{1,0:T(8,128)(2,1)S(1)} %get-tuple-element.44), channel_id=1, source_target_pairs={{0,6},{1,7},{2,4},{3,5},{4,2},{5,3},{6,0},{7,1},{8,14},{9,15},{10,... | collective-permute-start | bytes 393224 | tf_op jit(solution)/shard_map/ppermute | solution.py:185
  13.6 9.7 %collective-permute-start.1 = (bf16[128,512]{1,0:T(8,128)(2,1)S(1)}, bf16[128,512]{1,0:T(8,128)(2,1)S(1)}, u32[]{:S(2)}, u32[]{:S(2)}) collective-permute-start(bf16[128,512]{1,0:T(8,128)(2,1)S(1)} %get-tuple-element.44), channel_id=1, source_target_pairs={{0,2},{1,3},{2,0},{3,1},{4,6},{5,7},{6,4},{7,5},{8,10},{9,11},{10,... | collective-permute-start | bytes 393224 | tf_op jit(solution)/shard_map/ppermute | solution.py:185
  24.0 8.7 %collective-permute-start.4 = (bf16[128,512]{1,0:T(8,128)(2,1)S(1)}, bf16[128,512]{1,0:T(8,128)(2,1)S(1)}, u32[]{:S(2)}, u32[]{:S(2)}) collective-permute-start(bf16[128,512]{1,0:T(8,128)(2,1)S(1)} %get-tuple-element.45), channel_id=1, source_target_pairs={{0,8},{1,9},{2,10},{3,11},{4,12},{5,13},{6,14},{7,15},{8,16},{9,17... | collective-permute-start | bytes 393224 | tf_op jit(solution)/shard_map/ppermute | solution.py:195
  35.1 14.6 %collective-permute-start.9 = (bf16[128,512]{1,0:T(8,128)(2,1)S(1)}, bf16[128,512]{1,0:T(8,128)(2,1)S(1)}, u32[]{:S(2)}, u32[]{:S(2)}) collective-permute-start(bf16[128,512]{1,0:T(8,128)(2,1)S(1)} %get-tuple-element.47.refs_0_), channel_id=1, source_target_pairs={{0,4},{1,5},{2,6},{3,7},{4,0},{5,1},{6,2},{7,3},{8,12},{9,13},{10,... | collective-permute-start | bytes 393224 | tf_op jit(solution)/shard_map/ppermute | solution.py:185
  39.9 9.9 %collective-permute-start.10 = (bf16[128,512]{1,0:T(8,128)(2,1)S(1)}, bf16[128,512]{1,0:T(8,128)(2,1)S(1)}, u32[]{:S(2)}, u32[]{:S(2)}) collective-permute-start(bf16[128,512]{1,0:T(8,128)(2,1)S(1)} %get-tuple-element.48), channel_id=1, source_target_pairs={{0,6},{1,7},{2,4},{3,5},{4,2},{5,3},{6,0},{7,1},{8,14},{9,15},{10,... | collective-permute-start | bytes 393224 | tf_op jit(solution)/shard_map/ppermute | solution.py:185
  40.3 10.5 %collective-permute-start.8 = (bf16[128,512]{1,0:T(8,128)(2,1)S(1)}, bf16[128,512]{1,0:T(8,128)(2,1)S(1)}, u32[]{:S(2)}, u32[]{:S(2)}) collective-permute-start(bf16[128,512]{1,0:T(8,128)(2,1)S(1)} %get-tuple-element.48), channel_id=1, source_target_pairs={{0,2},{1,3},{2,0},{3,1},{4,6},{5,7},{6,4},{7,5},{8,10},{9,11},{10,... | collective-permute-start | bytes 393224 | tf_op jit(solution)/shard_map/ppermute | solution.py:185
  51.6 8.7 %collective-permute-start.11 = (bf16[128,512]{1,0:T(8,128)(2,1)S(1)}, bf16[128,512]{1,0:T(8,128)(2,1)S(1)}, u32[]{:S(2)}, u32[]{:S(2)}) collective-permute-start(bf16[128,512]{1,0:T(8,128)(2,1)S(1)} %get-tuple-element.49), channel_id=1, source_target_pairs={{0,8},{1,9},{2,10},{3,11},{4,12},{5,13},{6,14},{7,15},{8,16},{9,17... | collective-permute-start | bytes 393224 | tf_op jit(solution)/shard_map/ppermute | solution.py:195
  52.2 8.1 %collective-permute-start.12 = (bf16[128,512]{1,0:T(8,128)(2,1)S(1)}, bf16[128,512]{1,0:T(8,128)(2,1)S(1)}, u32[]{:S(2)}, u32[]{:S(2)}) collective-permute-start(bf16[128,512]{1,0:T(8,128)(2,1)S(1)} %get-tuple-element.50), channel_id=1, source_target_pairs={{0,10},{1,11},{2,8},{3,9},{4,14},{5,15},{6,12},{7,13},{8,18},{9,19... | collective-permute-start | bytes 393224 | tf_op jit(solution)/shard_map/ppermute | solution.py:195
  62.7 12.9 %collective-permute-start.16 = (bf16[128,512]{1,0:T(8,128)(2,1)S(1)}, bf16[128,512]{1,0:T(8,128)(2,1)S(1)}, u32[]{:S(2)}, u32[]{:S(2)}) collective-permute-start(bf16[128,512]{1,0:T(8,128)(2,1)S(1)} %get-tuple-element.51.refs_0_), channel_id=1, source_target_pairs={{0,4},{1,5},{2,6},{3,7},{4,0},{5,1},{6,2},{7,3},{8,12},{9,13},{10,... | collective-permute-start | bytes 393224 | tf_op jit(solution)/shard_map/ppermute | solution.py:185
  64.8 10.8 %collective-permute-start.17 = (bf16[128,512]{1,0:T(8,128)(2,1)S(1)}, bf16[128,512]{1,0:T(8,128)(2,1)S(1)}, u32[]{:S(2)}, u32[]{:S(2)}) collective-permute-start(bf16[128,512]{1,0:T(8,128)(2,1)S(1)} %get-tuple-element.52), channel_id=1, source_target_pairs={{0,6},{1,7},{2,4},{3,5},{4,2},{5,3},{6,0},{7,1},{8,14},{9,15},{10,... | collective-permute-start | bytes 393224 | tf_op jit(solution)/shard_map/ppermute | solution.py:185
  67.4 8.9 %collective-permute-start.15 = (bf16[128,512]{1,0:T(8,128)(2,1)S(1)}, bf16[128,512]{1,0:T(8,128)(2,1)S(1)}, u32[]{:S(2)}, u32[]{:S(2)}) collective-permute-start(bf16[128,512]{1,0:T(8,128)(2,1)S(1)} %get-tuple-element.52), channel_id=1, source_target_pairs={{0,2},{1,3},{2,0},{3,1},{4,6},{5,7},{6,4},{7,5},{8,10},{9,11},{10,... | collective-permute-start | bytes 393224 | tf_op jit(solution)/shard_map/ppermute | solution.py:185
  77.1 8.7 %collective-permute-start.18 = (bf16[128,512]{1,0:T(8,128)(2,1)S(1)}, bf16[128,512]{1,0:T(8,128)(2,1)S(1)}, u32[]{:S(2)}, u32[]{:S(2)}) collective-permute-start(bf16[128,512]{1,0:T(8,128)(2,1)S(1)} %get-tuple-element.53), channel_id=1, source_target_pairs={{0,8},{1,9},{2,10},{3,11},{4,12},{5,13},{6,14},{7,15},{8,16},{9,17... | collective-permute-start | bytes 393224 | tf_op jit(solution)/shard_map/ppermute | solution.py:195
  77.3 8.5 %collective-permute-start.19 = (bf16[128,512]{1,0:T(8,128)(2,1)S(1)}, bf16[128,512]{1,0:T(8,128)(2,1)S(1)}, u32[]{:S(2)}, u32[]{:S(2)}) collective-permute-start(bf16[128,512]{1,0:T(8,128)(2,1)S(1)} %get-tuple-element.54), channel_id=1, source_target_pairs={{0,10},{1,11},{2,8},{3,9},{4,14},{5,15},{6,12},{7,13},{8,18},{9,19... | collective-permute-start | bytes 393224 | tf_op jit(solution)/shard_map/ppermute | solution.py:195
  88.2 12.9 %collective-permute-start.23 = (bf16[128,512]{1,0:T(8,128)(2,1)S(1)}, bf16[128,512]{1,0:T(8,128)(2,1)S(1)}, u32[]{:S(2)}, u32[]{:S(2)}) collective-permute-start(bf16[128,512]{1,0:T(8,128)(2,1)S(1)} %get-tuple-element.55.refs_0_), channel_id=1, source_target_pairs={{0,4},{1,5},{2,6},{3,7},{4,0},{5,1},{6,2},{7,3},{8,12},{9,13},{10,... | collective-permute-start | bytes 393224 | tf_op jit(solution)/shard_map/ppermute | solution.py:185
  91.2 9.9 %collective-permute-start.24 = (bf16[128,512]{1,0:T(8,128)(2,1)S(1)}, bf16[128,512]{1,0:T(8,128)(2,1)S(1)}, u32[]{:S(2)}, u32[]{:S(2)}) collective-permute-start(bf16[128,512]{1,0:T(8,128)(2,1)S(1)} %get-tuple-element.56), channel_id=1, source_target_pairs={{0,6},{1,7},{2,4},{3,5},{4,2},{5,3},{6,0},{7,1},{8,14},{9,15},{10,... | collective-permute-start | bytes 393224 | tf_op jit(solution)/shard_map/ppermute | solution.py:185
  92.6 9.5 %collective-permute-start.22 = (bf16[128,512]{1,0:T(8,128)(2,1)S(1)}, bf16[128,512]{1,0:T(8,128)(2,1)S(1)}, u32[]{:S(2)}, u32[]{:S(2)}) collective-permute-start(bf16[128,512]{1,0:T(8,128)(2,1)S(1)} %get-tuple-element.56), channel_id=1, source_target_pairs={{0,2},{1,3},{2,0},{3,1},{4,6},{5,7},{6,4},{7,5},{8,10},{9,11},{10,... | collective-permute-start | bytes 393224 | tf_op jit(solution)/shard_map/ppermute | solution.py:185
  102.9 8.7 %collective-permute-start.25 = (bf16[128,512]{1,0:T(8,128)(2,1)S(1)}, bf16[128,512]{1,0:T(8,128)(2,1)S(1)}, u32[]{:S(2)}, u32[]{:S(2)}) collective-permute-start(bf16[128,512]{1,0:T(8,128)(2,1)S(1)} %get-tuple-element.57), channel_id=1, source_target_pairs={{0,8},{1,9},{2,10},{3,11},{4,12},{5,13},{6,14},{7,15},{8,16},{9,17... | collective-permute-start | bytes 393224 | tf_op jit(solution)/shard_map/ppermute | solution.py:195
  102.9 8.7 %collective-permute-start.26 = (bf16[128,512]{1,0:T(8,128)(2,1)S(1)}, bf16[128,512]{1,0:T(8,128)(2,1)S(1)}, u32[]{:S(2)}, u32[]{:S(2)}) collective-permute-start(bf16[128,512]{1,0:T(8,128)(2,1)S(1)} %get-tuple-element.58), channel_id=1, source_target_pairs={{0,10},{1,11},{2,8},{3,9},{4,14},{5,15},{6,12},{7,13},{8,18},{9,19... | collective-permute-start | bytes 393224 | tf_op jit(solution)/shard_map/ppermute | solution.py:195
  113.9 12.9 %collective-permute-start.30 = (bf16[128,512]{1,0:T(8,128)(2,1)S(1)}, bf16[128,512]{1,0:T(8,128)(2,1)S(1)}, u32[]{:S(2)}, u32[]{:S(2)}) collective-permute-start(bf16[128,512]{1,0:T(8,128)(2,1)S(1)} %get-tuple-element.59.refs_0_), channel_id=1, source_target_pairs={{0,4},{1,5},{2,6},{3,7},{4,0},{5,1},{6,2},{7,3},{8,12},{9,13},{10,... | collective-permute-start | bytes 393224 | tf_op jit(solution)/shard_map/ppermute | solution.py:185
  116.3 10.6 %collective-permute-start.31 = (bf16[128,512]{1,0:T(8,128)(2,1)S(1)}, bf16[128,512]{1,0:T(8,128)(2,1)S(1)}, u32[]{:S(2)}, u32[]{:S(2)}) collective-permute-start(bf16[128,512]{1,0:T(8,128)(2,1)S(1)} %get-tuple-element.60), channel_id=1, source_target_pairs={{0,6},{1,7},{2,4},{3,5},{4,2},{5,3},{6,0},{7,1},{8,14},{9,15},{10,... | collective-permute-start | bytes 393224 | tf_op jit(solution)/shard_map/ppermute | solution.py:185
  118.7 8.9 %collective-permute-start.29 = (bf16[128,512]{1,0:T(8,128)(2,1)S(1)}, bf16[128,512]{1,0:T(8,128)(2,1)S(1)}, u32[]{:S(2)}, u32[]{:S(2)}) collective-permute-start(bf16[128,512]{1,0:T(8,128)(2,1)S(1)} %get-tuple-element.60), channel_id=1, source_target_pairs={{0,2},{1,3},{2,0},{3,1},{4,6},{5,7},{6,4},{7,5},{8,10},{9,11},{10,... | collective-permute-start | bytes 393224 | tf_op jit(solution)/shard_map/ppermute | solution.py:185
  128.1 8.7 %collective-permute-start.32 = (bf16[128,512]{1,0:T(8,128)(2,1)S(1)}, bf16[128,512]{1,0:T(8,128)(2,1)S(1)}, u32[]{:S(2)}, u32[]{:S(2)}) collective-permute-start(bf16[128,512]{1,0:T(8,128)(2,1)S(1)} %get-tuple-element.61), channel_id=1, source_target_pairs={{0,8},{1,9},{2,10},{3,11},{4,12},{5,13},{6,14},{7,15},{8,16},{9,17... | collective-permute-start | bytes 393224 | tf_op jit(solution)/shard_map/ppermute | solution.py:195
  128.7 8.2 %collective-permute-start.33 = (bf16[128,512]{1,0:T(8,128)(2,1)S(1)}, bf16[128,512]{1,0:T(8,128)(2,1)S(1)}, u32[]{:S(2)}, u32[]{:S(2)}) collective-permute-start(bf16[128,512]{1,0:T(8,128)(2,1)S(1)} %get-tuple-element.62), channel_id=1, source_target_pairs={{0,10},{1,11},{2,8},{3,9},{4,14},{5,15},{6,12},{7,13},{8,18},{9,19... | collective-permute-start | bytes 393224 | tf_op jit(solution)/shard_map/ppermute | solution.py:195
  139.1 12.9 %collective-permute-start.37 = (bf16[128,512]{1,0:T(8,128)(2,1)S(1)}, bf16[128,512]{1,0:T(8,128)(2,1)S(1)}, u32[]{:S(2)}, u32[]{:S(2)}) collective-permute-start(bf16[128,512]{1,0:T(8,128)(2,1)S(1)} %get-tuple-element.63.refs_0_), channel_id=1, source_target_pairs={{0,4},{1,5},{2,6},{3,7},{4,0},{5,1},{6,2},{7,3},{8,12},{9,13},{10,... | collective-permute-start | bytes 393224 | tf_op jit(solution)/shard_map/ppermute | solution.py:185
  142.1 9.9 %collective-permute-start.38 = (bf16[128,512]{1,0:T(8,128)(2,1)S(1)}, bf16[128,512]{1,0:T(8,128)(2,1)S(1)}, u32[]{:S(2)}, u32[]{:S(2)}) collective-permute-start(bf16[128,512]{1,0:T(8,128)(2,1)S(1)} %get-tuple-element.64), channel_id=1, source_target_pairs={{0,6},{1,7},{2,4},{3,5},{4,2},{5,3},{6,0},{7,1},{8,14},{9,15},{10,... | collective-permute-start | bytes 393224 | tf_op jit(solution)/shard_map/ppermute | solution.py:185
  143.6 9.5 %collective-permute-start.36 = (bf16[128,512]{1,0:T(8,128)(2,1)S(1)}, bf16[128,512]{1,0:T(8,128)(2,1)S(1)}, u32[]{:S(2)}, u32[]{:S(2)}) collective-permute-start(bf16[128,512]{1,0:T(8,128)(2,1)S(1)} %get-tuple-element.64), channel_id=1, source_target_pairs={{0,2},{1,3},{2,0},{3,1},{4,6},{5,7},{6,4},{7,5},{8,10},{9,11},{10,... | collective-permute-start | bytes 393224 | tf_op jit(solution)/shard_map/ppermute | solution.py:185
  153.7 8.7 %collective-permute-start.39 = (bf16[128,512]{1,0:T(8,128)(2,1)S(1)}, bf16[128,512]{1,0:T(8,128)(2,1)S(1)}, u32[]{:S(2)}, u32[]{:S(2)}) collective-permute-start(bf16[128,512]{1,0:T(8,128)(2,1)S(1)} %get-tuple-element.65), channel_id=1, source_target_pairs={{0,8},{1,9},{2,10},{3,11},{4,12},{5,13},{6,14},{7,15},{8,16},{9,17... | collective-permute-start | bytes 393224 | tf_op jit(solution)/shard_map/ppermute | solution.py:195
  154.1 8.3 %collective-permute-start.40 = (bf16[128,512]{1,0:T(8,128)(2,1)S(1)}, bf16[128,512]{1,0:T(8,128)(2,1)S(1)}, u32[]{:S(2)}, u32[]{:S(2)}) collective-permute-start(bf16[128,512]{1,0:T(8,128)(2,1)S(1)} %get-tuple-element.66), channel_id=1, source_target_pairs={{0,10},{1,11},{2,8},{3,9},{4,14},{5,15},{6,12},{7,13},{8,18},{9,19... | collective-permute-start | bytes 393224 | tf_op jit(solution)/shard_map/ppermute | solution.py:195
  164.7 12.9 %collective-permute-start.44 = (bf16[128,512]{1,0:T(8,128)(2,1)S(1)}, bf16[128,512]{1,0:T(8,128)(2,1)S(1)}, u32[]{:S(2)}, u32[]{:S(2)}) collective-permute-start(bf16[128,512]{1,0:T(8,128)(2,1)S(1)} %get-tuple-element.67.refs_0_), channel_id=1, source_target_pairs={{0,4},{1,5},{2,6},{3,7},{4,0},{5,1},{6,2},{7,3},{8,12},{9,13},{10,... | collective-permute-start | bytes 393224 | tf_op jit(solution)/shard_map/ppermute | solution.py:185
  167.1 10.6 %collective-permute-start.45 = (bf16[128,512]{1,0:T(8,128)(2,1)S(1)}, bf16[128,512]{1,0:T(8,128)(2,1)S(1)}, u32[]{:S(2)}, u32[]{:S(2)}) collective-permute-start(bf16[128,512]{1,0:T(8,128)(2,1)S(1)} %get-tuple-element.68), channel_id=1, source_target_pairs={{0,6},{1,7},{2,4},{3,5},{4,2},{5,3},{6,0},{7,1},{8,14},{9,15},{10,... | collective-permute-start | bytes 393224 | tf_op jit(solution)/shard_map/ppermute | solution.py:185
  169.5 8.9 %collective-permute-start.43 = (bf16[128,512]{1,0:T(8,128)(2,1)S(1)}, bf16[128,512]{1,0:T(8,128)(2,1)S(1)}, u32[]{:S(2)}, u32[]{:S(2)}) collective-permute-start(bf16[128,512]{1,0:T(8,128)(2,1)S(1)} %get-tuple-element.68), channel_id=1, source_target_pairs={{0,2},{1,3},{2,0},{3,1},{4,6},{5,7},{6,4},{7,5},{8,10},{9,11},{10,... | collective-permute-start | bytes 393224 | tf_op jit(solution)/shard_map/ppermute | solution.py:185
  (16 other events, 36.8 us)
where the time goes:
time: 186 us
  waiting for transfers between devices  93.1 us (50%)
  starting transfers between devices  69.2 us (37%)
  Pallas kernels  19.8 us (11%)
  local copies, waits for them, and re-layouts  2.92 us (2%)
    ppermute x35, waiting for transfers between devices, along(): return lax.ppermute(value, 'blk', [(i, i ^ flip) for i in range(devices)])  70.6 us
    ppermute x35, starting transfers between devices, along(): return lax.ppermute(value, 'blk', [(i, i ^ flip) for i in range(devices)])  39.7 us
    ppermute x12, starting transfers between devices, passed(): lax.ppermute(part, ('segment', 'blk'), [(s * devices + i, (s + 1) % segme...  29.5 us
    ppermute x12, waiting for transfers between devices, passed(): lax.ppermute(part, ('segment', 'blk'), [(s * devices + i, (s + 1) % segme...  22.5 us
    pallas_call x14, Pallas kernels, layer(): pl.pallas_call(functools.partial(layer_kernel, len(pieces), outs, forward...  9.72 us
    pallas_call x2, Pallas kernels, placed_weights(): pl.pallas_call(functools.partial(place_kernel, layer, order), in_specs=[T...  8.19 us
  transfers between devices with their start and end apart: 47, of which 33 were waited for; matrix products, arithmetic and copies ran while one was open for 1% of the time, Pallas kernels for 5%

commit v1 on v0

v1 whole, which is shorter than its diff:
```python
import functools

import jax
import jax.numpy as jnp
from jax import lax
from jax.experimental import pallas as pl
from jax.experimental.pallas import tpu as pltpu
from jax.sharding import PartitionSpec as P

MIB = 1024 * 1024
PLACE_VMEM = 46 * MIB
LAYER_VMEM = 16 * MIB
WEIGHT_COPIES = 4
WHOLE = pl.BlockSpec(memory_space=pltpu.VMEM)
TABLE = pl.BlockSpec(memory_space=pltpu.SMEM)


def place_kernel(layer, order, column_ref, slot_ref, bias_ref, index_ref, weights_ref, placed_ref, row_ref, held, tile_ref, arrived, listed):
    slots, tile, width = held.shape
    lanes = 2 * tile
    copies = arrived.shape[0]
    per_copy = slots // copies
    pairs = slots // 2 // copies

    def copy(part):
        these = pl.ds(part * per_copy, per_copy)
        return pltpu.make_async_copy(weights_ref.at[layer, these], held.at[these], arrived.at[part])

    def place(pair):
        both_slots = [slot_ref[2 * pair], slot_ref[2 * pair + 1]]
        for block in range(width // lanes):
            columns = pl.ds(block * lanes, lanes)
            turned = jnp.concatenate([held[slot, :, columns] for slot in both_slots], axis=0).T
            for half in range(2):
                for side, slot in enumerate(both_slots):
                    row = pl.multiple_of(column_ref[layer, tile_ref[slot, 2 * block + half]] * tile, tile)
                    placed_ref[pair, pl.ds(row, tile), pl.ds(side * tile, tile)] = turned[
                        half * tile : (half + 1) * tile, side * tile : (side + 1) * tile
                    ]

    listing = pltpu.make_async_copy(index_ref.at[layer], tile_ref, listed)
    listing.start()
    for part in range(copies):
        copy(part).start()
    for spot in range(slots):
        row_ref[:, pl.ds(spot * tile, tile)] = bias_ref[layer, pl.ds(slot_ref[spot], 1), :]
    listing.wait()
    for part in range(copies):
        copy(part).wait()
        for pair in order[part * pairs : (part + 1) * pairs]:
            place(pair)


def placed(layer, weights, biases, tile_index, columns, slots_of, order):
    _, slots, tile, width = weights.shape
    copies = min(WEIGHT_COPIES, slots // 2)
    away = pl.BlockSpec(memory_space=pltpu.HBM)
    return pl.pallas_call(
        functools.partial(place_kernel, layer, order),
        in_specs=[TABLE, TABLE, WHOLE, away, away],
        out_specs=[WHOLE, WHOLE],
        out_shape=[
            jax.ShapeDtypeStruct((slots // 2, width, 2 * tile), weights.dtype),
            jax.ShapeDtypeStruct((1, slots * tile), biases.dtype),
        ],
        scratch_shapes=[
            pltpu.VMEM((slots, tile, width), weights.dtype),
            pltpu.SMEM(tile_index.shape[1:], tile_index.dtype),
            pltpu.SemaphoreType.DMA((copies,)),
            pltpu.SemaphoreType.DMA(()),
        ],
        compiler_params=pltpu.CompilerParams(vmem_limit_bytes=PLACE_VMEM),
        name="place_tiles",
    )(columns, slots_of, biases, tile_index, weights)


def turn_kernel(micro, *refs):
    for blocks_ref, turned_ref in zip(refs[: len(refs) // 2], refs[len(refs) // 2 :]):
        turned_ref[...] = blocks_ref[micro].T


def turned(arrays, micro):
    _, rows, columns = arrays[0].shape
    return pl.pallas_call(
        functools.partial(turn_kernel, micro),
        in_specs=[WHOLE] * len(arrays),
        out_specs=[WHOLE] * len(arrays),
        out_shape=[jax.ShapeDtypeStruct((columns, rows), arrays[0].dtype)] * len(arrays),
        compiler_params=pltpu.CompilerParams(vmem_limit_bytes=LAYER_VMEM),
        name="turn",
    )(*arrays)


def product(piece_refs, matrix_ref, first, step, depth):
    values = jnp.concatenate([piece[...] for piece in piece_refs], axis=1)
    rows = pl.ds(depth, values.shape[1])
    matrix = jnp.concatenate([matrix_ref[first + index, rows, :] for index in range(step)], axis=1)
    return jnp.dot(values, matrix, preferred_element_type=jnp.float32)


def early_kernel(*refs):
    *piece_refs, matrix_ref, offset_ref, total_ref = refs
    pairs, _, lanes = matrix_ref.shape
    step = 2 if pairs % 2 == 0 else 1
    for first in range(0, pairs, step):
        columns = pl.ds(first * lanes, step * lanes)
        total_ref[:, columns] = product(piece_refs, matrix_ref, first, step, 0) + offset_ref[:, columns]


def layer_kernel(pieces, parts, depth, forwarders, *refs):
    piece_refs, (matrix_ref, start_ref), refs = refs[:pieces], refs[pieces : pieces + 2], refs[pieces + 2 :]
    kept_refs, out_refs = refs[:-parts], refs[-parts:]
    pairs, _, lanes = matrix_ref.shape
    per_out = pairs // parts
    step = 2 if per_out % 2 == 0 else 1
    for first in range(0, pairs, step):
        total = product(piece_refs, matrix_ref, first, step, depth) + start_ref[:, pl.ds(first * lanes, step * lanes)]
        total = jnp.maximum(total, 0.0)
        part, columns = first // per_out, pl.ds(first % per_out * lanes, step * lanes)
        if kept_refs:
            place_ref, *held_refs = kept_refs
            hands_on = place_ref[0, :1, : step * lanes] < forwarders
            total = jnp.where(hands_on, held_refs[part][:, columns].astype(jnp.float32), total)
        out_refs[part][:, columns] = total.astype(out_refs[part].dtype)


def layer(pieces, matrix, offset, parts, late=0, place=None, forwarders=0, kept=()):
    pairs, width, lanes = matrix.shape
    batch, kind = pieces[0].shape[0], pieces[0].dtype
    outs = parts if pairs % parts == 0 else 1
    extra, kept = ([place], list(kept)) if forwarders else ([], [])
    early, pieces = (pieces[:-late], pieces[-late:]) if late else ([], pieces)
    if outs < parts:
        early, pieces, kept = [[jnp.concatenate(some, axis=1)] if some else [] for some in (early, pieces, kept)]
    params = pltpu.CompilerParams(vmem_limit_bytes=LAYER_VMEM)

    def cost(depth):
        flops, moved = 2 * batch * depth * pairs * lanes, 2 * pairs * depth * lanes
        return pl.CostEstimate(flops=flops, bytes_accessed=moved, transcendentals=0)

    depth = sum(piece.shape[1] for piece in early)
    start = offset
    if early:
        start = pl.pallas_call(
            early_kernel,
            in_specs=[WHOLE] * (len(early) + 2),
            out_specs=WHOLE,
            out_shape=jax.ShapeDtypeStruct((batch, pairs * lanes), jnp.float32),
            cost_estimate=cost(depth),
            compiler_params=params,
            name="layer_early",
        )(*early, matrix, offset)
    result = pl.pallas_call(
        functools.partial(layer_kernel, len(pieces), outs, depth, forwarders),
        in_specs=[WHOLE] * (len(pieces) + 2 + len(extra) + len(kept)),
        out_specs=[WHOLE] * outs,
        out_shape=[jax.ShapeDtypeStruct((batch, pairs * lanes // outs), kind)] * outs,
        cost_estimate=cost(width - depth),
        compiler_params=params,
        name="layer",
    )(*pieces, matrix, start, *extra, *kept)
    return list(result) if outs == parts else jnp.split(result[0], parts, axis=1)


def finish_kernel(place_ref, *refs):
    out_ref = refs[-1]
    deep, group, tile, batch = out_ref.shape
    part_refs, exchanged_refs = refs[:group], refs[group:-1]
    odd = place_ref[0, :1, :batch] % 2 == 1
    near = place_ref[1, :1, :batch]
    values = [part.T for part in [ref[...] for ref in part_refs]]
    for x in range(1, group):
        values[x] = jnp.where(odd, exchanged_refs[x - 1][...].T, values[x])
    for e in range(group):
        value = values[e]
        for digit in range(1, group):
            value = jnp.where(near == digit, values[e ^ digit], value)
        out_ref[:, e] = value.reshape(deep, tile, batch)


def finished(parts, exchanged, place, shape):
    return pl.pallas_call(
        finish_kernel,
        in_specs=[WHOLE] * (1 + len(parts) + len(exchanged)),
        out_specs=WHOLE,
        out_shape=jax.ShapeDtypeStruct(shape, parts[0].dtype),
        compiler_params=pltpu.CompilerParams(vmem_limit_bytes=LAYER_VMEM),
        name="finish",
    )(place, *parts, *exchanged)


def body(inputs, weights, biases, tile_index):
    micro_count, local, tile, batch = inputs.shape
    fan = tile_index.shape[2]
    segments, devices = lax.axis_size("segment"), lax.axis_size("blk")
    assert micro_count == segments and segments % 2 == 0
    group = min(local, devices // 4)
    deep = local // group
    part_width = deep * tile
    segment, position = lax.axis_index("segment"), lax.axis_index("blk")
    core, near, far = position & 1, (position >> 1) & (group - 1), position // (2 * group) & 1

    member = jnp.arange(fan, dtype=jnp.int32)
    member_digit, member_slot = member // local, member % local
    in_part = ((member_slot % group) ^ near) * deep + member_slot // group
    even_columns = (member_digit ^ core) * local + jnp.where(segment == 0, member_slot, in_part)
    part, across = (member_slot % group) ^ near, member_digit ^ far
    odd_piece = jnp.where(across == 0, jnp.where(part == 0, 0, 1 + part), jnp.where(part == 0, 1, group + part))
    odd_columns = odd_piece * deep + member_slot // group
    columns = jnp.stack([even_columns, odd_columns])
    spot = jnp.arange(local, dtype=jnp.int32)
    slots_of = spot % deep * group + ((spot // deep) ^ near)
    first_of = [(2 * pair) % deep * group if deep > 1 else 2 * pair for pair in range(local // 2)]
    order = sorted(range(local // 2), key=lambda pair: (first_of[pair], pair))
    place = jnp.broadcast_to(jnp.stack([segment, near]).astype(jnp.int32)[:, None, None], (2, 8, max(batch, 4 * tile)))
    columns, slots_of, place, first = lax.optimization_barrier((columns, slots_of, place, segment == 0))
    layers = [placed(index, weights, biases, tile_index, columns, slots_of, order) for index in range(2)]

    def along(value, flip):
        return lax.ppermute(value, "blk", [(i, i ^ flip) for i in range(devices)])

    def exchange(parts):
        pieces = {0: parts[0]}
        for x in range(1, 2 * group):
            pieces[x] = along(parts[x % group], 2 * x)
        return [pieces[x] for x in (0, group, *range(1, group), *range(group + 1, 2 * group))]

    def passed(parts):
        return [
            lax.ppermute(
                part,
                ("segment", "blk"),
                [(s * devices + i, (s + 1) % segments * devices + (i ^ 2 * x)) for s in range(segments) for i in range(devices)],
            )
            for x, part in enumerate(parts)
        ]

    sequence = [*range(segments - 2, -1, -1), segments - 1]
    turns = micro_count + segments - 1
    fresh = inputs.reshape(micro_count, local * tile, batch)
    arriving = ()
    for turn in range(turns):
        if turn == 0:
            pieces = turned([fresh, along(fresh, 1)], sequence[turn])
        elif turn < micro_count:
            (new,) = turned([fresh], sequence[turn])
            new = [new[:, x * part_width : (x + 1) * part_width] for x in range(group)]
            pieces = [jnp.where(first, a, b) for a, b in zip(new, arriving)]
        else:
            pieces = arriving
        if turn:
            pieces = pieces + [along(part, 1) for part in pieces]
        parts = layer(pieces, *layers[0], group, 1 if turn else 0)
        pieces = exchange(parts)
        forwarders = max(0, turn - micro_count + 1)
        parts = layer(pieces, *layers[1], group, 1, place, forwarders, arriving)
        if turn < turns - 1:
            arriving = passed(parts)

    exchanged = [along(parts[x], 2 * x) for x in range(1, group)]
    return finished(parts, exchanged, place, (deep, group, tile, batch)).reshape(1, local, tile, batch)


def solution(mesh):
    in_specs = (
        P(None, "blk", None, None),
        P("segment", "blk", None, None),
        P("segment", "blk", None),
        P("segment", "blk", None),
    )
    out_specs = P("segment", "blk", None, None)
    return jax.shard_map(body, mesh=mesh, in_specs=in_specs, out_specs=out_specs, check_vma=False)
```

time: 186 us -> 179 us (0.962)
  starting transfers between devices: 69.2 us -> 65.5 us
  waiting for transfers between devices: 93.1 us -> 89.5 us
  Pallas kernels: 19.8 us -> 22 us
    ppermute x35, waiting for transfers between devices: 70.6 us -> 64.9 us  [along(): return lax.ppermute(value, 'blk', [(i, i ^ flip) for i in range(devices)])]
    ppermute x12, starting transfers between devices: 29.5 us -> 26.2 us  [passed(): lax.ppermute(part, ('segment', 'blk'), [(s * devices + i, (s + 1) % segme...]
    pallas_call x21 -> x34, Pallas kernels: 19.8 us -> 22 us  [the longest x13 8.08 us: layer(): pl.pallas_call(early_kernel, in_specs=[WHOLE] * (len(early) + 2), out_spe...]
    ppermute x12, waiting for transfers between devices: 22.5 us -> 24.6 us  [passed(): lax.ppermute(part, ('segment', 'blk'), [(s * devices + i, (s + 1) % segme...]
  transfers between devices with their start and end apart: 47 -> 47, of which waited for: 33 -> 28; matrix products, arithmetic and copies ran while one was open for 1% -> 0% of each run, Pallas kernels for 5% -> 9%
where the time goes in v1:
time: 179 us
  waiting for transfers between devices  89.5 us (50%)
  starting transfers between devices  65.5 us (37%)
  Pallas kernels  22 us (12%)
    ppermute x35, waiting for transfers between devices, along(): return lax.ppermute(value, 'blk', [(i, i ^ flip) for i in range(devices)])  64.9 us
    ppermute x35, starting transfers between devices, along(): return lax.ppermute(value, 'blk', [(i, i ^ flip) for i in range(devices)])  39.3 us
    ppermute x12, starting transfers between devices, passed(): lax.ppermute(part, ('segment', 'blk'), [(s * devices + i, (s + 1) % segme...  26.2 us
    ppermute x12, waiting for transfers between devices, passed(): lax.ppermute(part, ('segment', 'blk'), [(s * devices + i, (s + 1) % segme...  24.6 us
    pallas_call x13, Pallas kernels, layer(): pl.pallas_call(early_kernel, in_specs=[WHOLE] * (len(early) + 2), out_spe...  8.08 us
    pallas_call x2, Pallas kernels, placed(): pl.pallas_call(functools.partial(place_kernel, layer, order), in_specs=[T...  7.7 us
    pallas_call x14, Pallas kernels, layer(): pl.pallas_call(functools.partial(layer_kernel, len(pieces), outs, depth,...  4.81 us
  transfers between devices with their start and end apart: 47, of which 28 were waited for; matrix products, arithmetic and copies ran while one was open for 0% of the time, Pallas kernels for 9%

profile of v1, /device:TPU:0, one launch (start us, length us, event | category | flops | bytes accessed | tf_op | source)
XLA Modules:
  0.0 179.1 jit_solution(14871432728537036218)
XLA Ops:
  2.1 3.6 %place_tiles.2 = (bf16[8,2048,128]{2,1,0:T(8,128)(2,1)S(1)}, f32[1,1024]{1,0:T(1,128)S(1)}) custom-call(s32[2,32]{1,0:T(2,128)S(1)} %pad_add_fusion.column_ref, s32[16]{0:T(128)S(1)} %fusion.3.slot_ref, f32[2,16,64]{2,1,0:T(8,128)S(1)} %copy-done.1, s32[2,16,32]{2,1,0:T(8,128)S(1)} %copy-done.2, bf16[2,16,64,2048]{3,2,1,0:T(8,128)(2,1)} %weights_ref.3), custom_call_target="tpu_custom_call" | custom-call | tf_op jit(solution)/shard_map/place_tiles/pallas_call | solution.py:58
  6.7 3.7 %collective-permute-start.2 = (bf16[128,512]{1,0:T(8,128)(2,1)S(1)}, bf16[128,512]{1,0:T(8,128)(2,1)S(1)}, u32[]{:S(2)}, u32[]{:S(2)}) collective-permute-start(bf16[128,512]{1,0:T(8,128)(2,1)S(1)} %get-tuple-element.53.refs_0_), channel_id=1, source_target_pairs={{0,4},{1,5},{2,6},{3,7},{4,0},{5,1},{6,2},{7,3},{8,12},{9,13},{10,... | collective-permute-start | bytes 393224 | tf_op jit(solution)/shard_map/ppermute | solution.py:220
  11.9 4.1 %place_tiles.3 = (bf16[8,2048,128]{2,1,0:T(8,128)(2,1)S(1)}, f32[1,1024]{1,0:T(1,128)S(1)}) custom-call(s32[2,32]{1,0:T(2,128)S(1)} %pad_add_fusion.column_ref, s32[16]{0:T(128)S(1)} %fusion.3.slot_ref, f32[2,16,64]{2,1,0:T(8,128)S(1)} %copy-done.1, s32[2,16,32]{2,1,0:T(8,128)S(1)} %copy-done.2, bf16[2,16,64,2048]{3,2,1,0:T(8,128)(2,1)} %weights_ref.3), custom_call_target="tpu_custom_call" | custom-call | tf_op jit(solution)/shard_map/place_tiles/pallas_call | solution.py:58
  18.3 3.1 %collective-permute-done.1.refs_0_ = bf16[128,512]{1,0:T(8,128)(2,1)S(1)} collective-permute-done((bf16[128,512]{1,0:T(8,128)(2,1)S(1)}, bf16[128,512]{1,0:T(8,128)(2,1)S(1)}, u32[]{:S(2)}, u32[]{:S(2)}) %collective-permute-start.1) | collective-permute-done | bytes 131104 | tf_op jit(solution)/shard_map/ppermute | solution.py:220
  23.2 3.3 %collective-permute-start.4 = (bf16[128,512]{1,0:T(8,128)(2,1)S(1)}, bf16[128,512]{1,0:T(8,128)(2,1)S(1)}, u32[]{:S(2)}, u32[]{:S(2)}) collective-permute-start(bf16[128,512]{1,0:T(8,128)(2,1)S(1)} %get-tuple-element.55), channel_id=1, source_target_pairs={{0,10},{1,11},{2,8},{3,9},{4,14},{5,15},{6,12},{7,13},{8,18},{9,19... | collective-permute-start | bytes 393224 | tf_op jit(solution)/shard_map/ppermute | solution.py:230
  26.6 3.9 %collective-permute-done.6 = bf16[128,512]{1,0:T(8,128)(2,1)S(1)} collective-permute-done((bf16[128,512]{1,0:T(8,128)(2,1)S(1)}, bf16[128,512]{1,0:T(8,128)(2,1)S(1)}, u32[]{:S(2)}, u32[]{:S(2)}) %collective-permute-start.6) | collective-permute-done | bytes 131104 | tf_op jit(solution)/shard_map/ppermute | solution.py:230
  32.9 4.7 %collective-permute-start.9 = (bf16[128,512]{1,0:T(8,128)(2,1)S(1)}, bf16[128,512]{1,0:T(8,128)(2,1)S(1)}, u32[]{:S(2)}, u32[]{:S(2)}) collective-permute-start(bf16[128,512]{1,0:T(8,128)(2,1)S(1)} %get-tuple-element.58.refs_0_), channel_id=1, source_target_pairs={{0,4},{1,5},{2,6},{3,7},{4,0},{5,1},{6,2},{7,3},{8,12},{9,13},{10,... | collective-permute-start | bytes 393224 | tf_op jit(solution)/shard_map/ppermute | solution.py:220
  39.2 6.2 %collective-permute-done.9.refs_1_ = bf16[128,512]{1,0:T(8,128)(2,1)S(1)} collective-permute-done((bf16[128,512]{1,0:T(8,128)(2,1)S(1)}, bf16[128,512]{1,0:T(8,128)(2,1)S(1)}, u32[]{:S(2)}, u32[]{:S(2)}) %collective-permute-start.9) | collective-permute-done | bytes 131104 | tf_op jit(solution)/shard_map/ppermute | solution.py:220
  45.3 2.9 %collective-permute-done.10.refs_2_ = bf16[128,512]{1,0:T(8,128)(2,1)S(1)} collective-permute-done((bf16[128,512]{1,0:T(8,128)(2,1)S(1)}, bf16[128,512]{1,0:T(8,128)(2,1)S(1)}, u32[]{:S(2)}, u32[]{:S(2)}) %collective-permute-start.10) | collective-permute-done | bytes 131104 | tf_op jit(solution)/shard_map/ppermute | solution.py:220
  49.9 3.4 %collective-permute-start.11 = (bf16[128,512]{1,0:T(8,128)(2,1)S(1)}, bf16[128,512]{1,0:T(8,128)(2,1)S(1)}, u32[]{:S(2)}, u32[]{:S(2)}) collective-permute-start(bf16[128,512]{1,0:T(8,128)(2,1)S(1)} %get-tuple-element.59), channel_id=1, source_target_pairs={{0,10},{1,11},{2,8},{3,9},{4,14},{5,15},{6,12},{7,13},{8,18},{9,19... | collective-permute-start | bytes 393224 | tf_op jit(solution)/shard_map/ppermute | solution.py:230
  53.4 4.5 %collective-permute-done.13 = bf16[128,512]{1,0:T(8,128)(2,1)S(1)} collective-permute-done((bf16[128,512]{1,0:T(8,128)(2,1)S(1)}, bf16[128,512]{1,0:T(8,128)(2,1)S(1)}, u32[]{:S(2)}, u32[]{:S(2)}) %collective-permute-start.13) | collective-permute-done | bytes 131104 | tf_op jit(solution)/shard_map/ppermute | solution.py:230
  64.7 5.9 %collective-permute-done.16.refs_1_ = bf16[128,512]{1,0:T(8,128)(2,1)S(1)} collective-permute-done((bf16[128,512]{1,0:T(8,128)(2,1)S(1)}, bf16[128,512]{1,0:T(8,128)(2,1)S(1)}, u32[]{:S(2)}, u32[]{:S(2)}) %collective-permute-start.16) | collective-permute-done | bytes 131104 | tf_op jit(solution)/shard_map/ppermute | solution.py:220
  71.2 2.7 %collective-permute-done.15.refs_0_ = bf16[128,512]{1,0:T(8,128)(2,1)S(1)} collective-permute-done((bf16[128,512]{1,0:T(8,128)(2,1)S(1)}, bf16[128,512]{1,0:T(8,128)(2,1)S(1)}, u32[]{:S(2)}, u32[]{:S(2)}) %collective-permute-start.15) | collective-permute-done | bytes 131104 | tf_op jit(solution)/shard_map/ppermute | solution.py:220
  74.3 4.3 %collective-permute-start.18 = (bf16[128,512]{1,0:T(8,128)(2,1)S(1)}, bf16[128,512]{1,0:T(8,128)(2,1)S(1)}, u32[]{:S(2)}, u32[]{:S(2)}) collective-permute-start(bf16[128,512]{1,0:T(8,128)(2,1)S(1)} %get-tuple-element.63), channel_id=1, source_target_pairs={{0,10},{1,11},{2,8},{3,9},{4,14},{5,15},{6,12},{7,13},{8,18},{9,19... | collective-permute-start | bytes 393224 | tf_op jit(solution)/shard_map/ppermute | solution.py:230
  78.7 4.0 %collective-permute-done.20 = bf16[128,512]{1,0:T(8,128)(2,1)S(1)} collective-permute-done((bf16[128,512]{1,0:T(8,128)(2,1)S(1)}, bf16[128,512]{1,0:T(8,128)(2,1)S(1)}, u32[]{:S(2)}, u32[]{:S(2)}) %collective-permute-start.20) | collective-permute-done | bytes 131104 | tf_op jit(solution)/shard_map/ppermute | solution.py:230
  85.1 2.8 %collective-permute-start.23 = (bf16[128,512]{1,0:T(8,128)(2,1)S(1)}, bf16[128,512]{1,0:T(8,128)(2,1)S(1)}, u32[]{:S(2)}, u32[]{:S(2)}) collective-permute-start(bf16[128,512]{1,0:T(8,128)(2,1)S(1)} %get-tuple-element.66.refs_0_), channel_id=1, source_target_pairs={{0,4},{1,5},{2,6},{3,7},{4,0},{5,1},{6,2},{7,3},{8,12},{9,13},{10,... | collective-permute-start | bytes 393224 | tf_op jit(solution)/shard_map/ppermute | solution.py:220
  89.5 5.8 %collective-permute-done.23.refs_1_ = bf16[128,512]{1,0:T(8,128)(2,1)S(1)} collective-permute-done((bf16[128,512]{1,0:T(8,128)(2,1)S(1)}, bf16[128,512]{1,0:T(8,128)(2,1)S(1)}, u32[]{:S(2)}, u32[]{:S(2)}) %collective-permute-start.23) | collective-permute-done | bytes 131104 | tf_op jit(solution)/shard_map/ppermute | solution.py:220
  96.0 2.7 %collective-permute-done.22.refs_0_ = bf16[128,512]{1,0:T(8,128)(2,1)S(1)} collective-permute-done((bf16[128,512]{1,0:T(8,128)(2,1)S(1)}, bf16[128,512]{1,0:T(8,128)(2,1)S(1)}, u32[]{:S(2)}, u32[]{:S(2)}) %collective-permute-start.22) | collective-permute-done | bytes 131104 | tf_op jit(solution)/shard_map/ppermute | solution.py:220
  99.5 3.9 %collective-permute-start.25 = (bf16[128,512]{1,0:T(8,128)(2,1)S(1)}, bf16[128,512]{1,0:T(8,128)(2,1)S(1)}, u32[]{:S(2)}, u32[]{:S(2)}) collective-permute-start(bf16[128,512]{1,0:T(8,128)(2,1)S(1)} %get-tuple-element.67), channel_id=1, source_target_pairs={{0,10},{1,11},{2,8},{3,9},{4,14},{5,15},{6,12},{7,13},{8,18},{9,19... | collective-permute-start | bytes 393224 | tf_op jit(solution)/shard_map/ppermute | solution.py:230
  103.4 4.1 %collective-permute-done.27.refs_0_.refs_4_ = bf16[128,512]{1,0:T(8,128)(2,1)S(1)} collective-permute-done((bf16[128,512]{1,0:T(8,128)(2,1)S(1)}, bf16[128,512]{1,0:T(8,128)(2,1)S(1)}, u32[]{:S(2)}, u32[]{:S(2)}) %collective-permute-start.27) | collective-permute-done | bytes 131104 | tf_op jit(solution)/shard_map/ppermute | solution.py:230
  114.3 5.8 %collective-permute-done.30.refs_1_ = bf16[128,512]{1,0:T(8,128)(2,1)S(1)} collective-permute-done((bf16[128,512]{1,0:T(8,128)(2,1)S(1)}, bf16[128,512]{1,0:T(8,128)(2,1)S(1)}, u32[]{:S(2)}, u32[]{:S(2)}) %collective-permute-start.30) | collective-permute-done | bytes 131104 | tf_op jit(solution)/shard_map/ppermute | solution.py:220
  120.7 2.8 %collective-permute-done.29.refs_0_ = bf16[128,512]{1,0:T(8,128)(2,1)S(1)} collective-permute-done((bf16[128,512]{1,0:T(8,128)(2,1)S(1)}, bf16[128,512]{1,0:T(8,128)(2,1)S(1)}, u32[]{:S(2)}, u32[]{:S(2)}) %collective-permute-start.29) | collective-permute-done | bytes 131104 | tf_op jit(solution)/shard_map/ppermute | solution.py:220
  123.9 4.2 %collective-permute-start.32 = (bf16[128,512]{1,0:T(8,128)(2,1)S(1)}, bf16[128,512]{1,0:T(8,128)(2,1)S(1)}, u32[]{:S(2)}, u32[]{:S(2)}) collective-permute-start(bf16[128,512]{1,0:T(8,128)(2,1)S(1)} %get-tuple-element.71), channel_id=1, source_target_pairs={{0,10},{1,11},{2,8},{3,9},{4,14},{5,15},{6,12},{7,13},{8,18},{9,19... | collective-permute-start | bytes 393224 | tf_op jit(solution)/shard_map/ppermute | solution.py:230
  128.1 4.1 %collective-permute-done.34.refs_0_.refs_4_ = bf16[128,512]{1,0:T(8,128)(2,1)S(1)} collective-permute-done((bf16[128,512]{1,0:T(8,128)(2,1)S(1)}, bf16[128,512]{1,0:T(8,128)(2,1)S(1)}, u32[]{:S(2)}, u32[]{:S(2)}) %collective-permute-start.34) | collective-permute-done | bytes 131104 | tf_op jit(solution)/shard_map/ppermute | solution.py:230
  134.6 2.7 %collective-permute-start.37 = (bf16[128,512]{1,0:T(8,128)(2,1)S(1)}, bf16[128,512]{1,0:T(8,128)(2,1)S(1)}, u32[]{:S(2)}, u32[]{:S(2)}) collective-permute-start(bf16[128,512]{1,0:T(8,128)(2,1)S(1)} %get-tuple-element.74.refs_0_), channel_id=1, source_target_pairs={{0,4},{1,5},{2,6},{3,7},{4,0},{5,1},{6,2},{7,3},{8,12},{9,13},{10,... | collective-permute-start | bytes 393224 | tf_op jit(solution)/shard_map/ppermute | solution.py:220
  139.0 5.9 %collective-permute-done.37.refs_1_ = bf16[128,512]{1,0:T(8,128)(2,1)S(1)} collective-permute-done((bf16[128,512]{1,0:T(8,128)(2,1)S(1)}, bf16[128,512]{1,0:T(8,128)(2,1)S(1)}, u32[]{:S(2)}, u32[]{:S(2)}) %collective-permute-start.37) | collective-permute-done | bytes 131104 | tf_op jit(solution)/shard_map/ppermute | solution.py:220
  148.6 4.3 %collective-permute-start.39 = (bf16[128,512]{1,0:T(8,128)(2,1)S(1)}, bf16[128,512]{1,0:T(8,128)(2,1)S(1)}, u32[]{:S(2)}, u32[]{:S(2)}) collective-permute-start(bf16[128,512]{1,0:T(8,128)(2,1)S(1)} %get-tuple-element.75), channel_id=1, source_target_pairs={{0,10},{1,11},{2,8},{3,9},{4,14},{5,15},{6,12},{7,13},{8,18},{9,19... | collective-permute-start | bytes 393224 | tf_op jit(solution)/shard_map/ppermute | solution.py:230
  152.9 4.1 %collective-permute-done.41.refs_0_.refs_4_ = bf16[128,512]{1,0:T(8,128)(2,1)S(1)} collective-permute-done((bf16[128,512]{1,0:T(8,128)(2,1)S(1)}, bf16[128,512]{1,0:T(8,128)(2,1)S(1)}, u32[]{:S(2)}, u32[]{:S(2)}) %collective-permute-start.41) | collective-permute-done | bytes 131104 | tf_op jit(solution)/shard_map/ppermute | solution.py:230
  159.2 2.7 %collective-permute-start.44 = (bf16[128,512]{1,0:T(8,128)(2,1)S(1)}, bf16[128,512]{1,0:T(8,128)(2,1)S(1)}, u32[]{:S(2)}, u32[]{:S(2)}) collective-permute-start(bf16[128,512]{1,0:T(8,128)(2,1)S(1)} %get-tuple-element.78.refs_0_), channel_id=1, source_target_pairs={{0,4},{1,5},{2,6},{3,7},{4,0},{5,1},{6,2},{7,3},{8,12},{9,13},{10,... | collective-permute-start | bytes 393224 | tf_op jit(solution)/shard_map/ppermute | solution.py:220
  163.7 5.8 %collective-permute-done.44.refs_1_ = bf16[128,512]{1,0:T(8,128)(2,1)S(1)} collective-permute-done((bf16[128,512]{1,0:T(8,128)(2,1)S(1)}, bf16[128,512]{1,0:T(8,128)(2,1)S(1)}, u32[]{:S(2)}, u32[]{:S(2)}) %collective-permute-start.44) | collective-permute-done | bytes 131104 | tf_op jit(solution)/shard_map/ppermute | solution.py:220
  170.1 2.8 %collective-permute-done.43.refs_0_ = bf16[128,512]{1,0:T(8,128)(2,1)S(1)} collective-permute-done((bf16[128,512]{1,0:T(8,128)(2,1)S(1)}, bf16[128,512]{1,0:T(8,128)(2,1)S(1)}, u32[]{:S(2)}, u32[]{:S(2)}) %collective-permute-start.43) | collective-permute-done | bytes 131104 | tf_op jit(solution)/shard_map/ppermute | solution.py:220
  175.1 3.1 %collective-permute-done.46.refs_2_ = bf16[128,512]{1,0:T(8,128)(2,1)S(1)} collective-permute-done((bf16[128,512]{1,0:T(8,128)(2,1)S(1)}, bf16[128,512]{1,0:T(8,128)(2,1)S(1)}, u32[]{:S(2)}, u32[]{:S(2)}) %collective-permute-start.46) | collective-permute-done | bytes 131104 | tf_op jit(solution)/shard_map/ppermute | solution.py:220
  (110 shorter events, 51.1 us)
Async XLA Ops:
  6.7 10.9 %collective-permute-start.2 = (bf16[128,512]{1,0:T(8,128)(2,1)S(1)}, bf16[128,512]{1,0:T(8,128)(2,1)S(1)}, u32[]{:S(2)}, u32[]{:S(2)}) collective-permute-start(bf16[128,512]{1,0:T(8,128)(2,1)S(1)} %get-tuple-element.53.refs_0_), channel_id=1, source_target_pairs={{0,4},{1,5},{2,6},{3,7},{4,0},{5,1},{6,2},{7,3},{8,12},{9,13},{10,... | collective-permute-start | bytes 393224 | tf_op jit(solution)/shard_map/ppermute | solution.py:220
  11.9 9.4 %collective-permute-start.1 = (bf16[128,512]{1,0:T(8,128)(2,1)S(1)}, bf16[128,512]{1,0:T(8,128)(2,1)S(1)}, u32[]{:S(2)}, u32[]{:S(2)}) collective-permute-start(bf16[128,512]{1,0:T(8,128)(2,1)S(1)} %get-tuple-element.51), channel_id=1, source_target_pairs={{0,6},{1,7},{2,4},{3,5},{4,2},{5,3},{6,0},{7,1},{8,14},{9,15},{10,... | collective-permute-start | bytes 393224 | tf_op jit(solution)/shard_map/ppermute | solution.py:220
  21.7 8.8 %collective-permute-start.6 = (bf16[128,512]{1,0:T(8,128)(2,1)S(1)}, bf16[128,512]{1,0:T(8,128)(2,1)S(1)}, u32[]{:S(2)}, u32[]{:S(2)}) collective-permute-start(bf16[128,512]{1,0:T(8,128)(2,1)S(1)} %get-tuple-element.56), channel_id=1, source_target_pairs={{0,8},{1,9},{2,10},{3,11},{4,12},{5,13},{6,14},{7,15},{8,16},{9,17... | collective-permute-start | bytes 393224 | tf_op jit(solution)/shard_map/ppermute | solution.py:230
  23.2 7.3 %collective-permute-start.4 = (bf16[128,512]{1,0:T(8,128)(2,1)S(1)}, bf16[128,512]{1,0:T(8,128)(2,1)S(1)}, u32[]{:S(2)}, u32[]{:S(2)}) collective-permute-start(bf16[128,512]{1,0:T(8,128)(2,1)S(1)} %get-tuple-element.55), channel_id=1, source_target_pairs={{0,10},{1,11},{2,8},{3,9},{4,14},{5,15},{6,12},{7,13},{8,18},{9,19... | collective-permute-start | bytes 393224 | tf_op jit(solution)/shard_map/ppermute | solution.py:230
  32.9 12.4 %collective-permute-start.9 = (bf16[128,512]{1,0:T(8,128)(2,1)S(1)}, bf16[128,512]{1,0:T(8,128)(2,1)S(1)}, u32[]{:S(2)}, u32[]{:S(2)}) collective-permute-start(bf16[128,512]{1,0:T(8,128)(2,1)S(1)} %get-tuple-element.58.refs_0_), channel_id=1, source_target_pairs={{0,4},{1,5},{2,6},{3,7},{4,0},{5,1},{6,2},{7,3},{8,12},{9,13},{10,... | collective-permute-start | bytes 393224 | tf_op jit(solution)/shard_map/ppermute | solution.py:220
  37.6 10.6 %collective-permute-start.10 = (bf16[128,512]{1,0:T(8,128)(2,1)S(1)}, bf16[128,512]{1,0:T(8,128)(2,1)S(1)}, u32[]{:S(2)}, u32[]{:S(2)}) collective-permute-start(bf16[128,512]{1,0:T(8,128)(2,1)S(1)} %get-tuple-element.57), channel_id=1, source_target_pairs={{0,2},{1,3},{2,0},{3,1},{4,6},{5,7},{6,4},{7,5},{8,10},{9,11},{10,... | collective-permute-start | bytes 393224 | tf_op jit(solution)/shard_map/ppermute | solution.py:220
  37.6 11.3 %collective-permute-start.8 = (bf16[128,512]{1,0:T(8,128)(2,1)S(1)}, bf16[128,512]{1,0:T(8,128)(2,1)S(1)}, u32[]{:S(2)}, u32[]{:S(2)}) collective-permute-start(bf16[128,512]{1,0:T(8,128)(2,1)S(1)} %get-tuple-element.57), channel_id=1, source_target_pairs={{0,6},{1,7},{2,4},{3,5},{4,2},{5,3},{6,0},{7,1},{8,14},{9,15},{10,... | collective-permute-start | bytes 393224 | tf_op jit(solution)/shard_map/ppermute | solution.py:220
  49.2 8.6 %collective-permute-start.13 = (bf16[128,512]{1,0:T(8,128)(2,1)S(1)}, bf16[128,512]{1,0:T(8,128)(2,1)S(1)}, u32[]{:S(2)}, u32[]{:S(2)}) collective-permute-start(bf16[128,512]{1,0:T(8,128)(2,1)S(1)} %get-tuple-element.60), channel_id=1, source_target_pairs={{0,8},{1,9},{2,10},{3,11},{4,12},{5,13},{6,14},{7,15},{8,16},{9,17... | collective-permute-start | bytes 393224 | tf_op jit(solution)/shard_map/ppermute | solution.py:230
  49.9 8.0 %collective-permute-start.11 = (bf16[128,512]{1,0:T(8,128)(2,1)S(1)}, bf16[128,512]{1,0:T(8,128)(2,1)S(1)}, u32[]{:S(2)}, u32[]{:S(2)}) collective-permute-start(bf16[128,512]{1,0:T(8,128)(2,1)S(1)} %get-tuple-element.59), channel_id=1, source_target_pairs={{0,10},{1,11},{2,8},{3,9},{4,14},{5,15},{6,12},{7,13},{8,18},{9,19... | collective-permute-start | bytes 393224 | tf_op jit(solution)/shard_map/ppermute | solution.py:230
  60.3 10.3 %collective-permute-start.16 = (bf16[128,512]{1,0:T(8,128)(2,1)S(1)}, bf16[128,512]{1,0:T(8,128)(2,1)S(1)}, u32[]{:S(2)}, u32[]{:S(2)}) collective-permute-start(bf16[128,512]{1,0:T(8,128)(2,1)S(1)} %get-tuple-element.62.refs_0_), channel_id=1, source_target_pairs={{0,4},{1,5},{2,6},{3,7},{4,0},{5,1},{6,2},{7,3},{8,12},{9,13},{10,... | collective-permute-start | bytes 393224 | tf_op jit(solution)/shard_map/ppermute | solution.py:220
  61.3 9.3 %collective-permute-start.17 = (bf16[128,512]{1,0:T(8,128)(2,1)S(1)}, bf16[128,512]{1,0:T(8,128)(2,1)S(1)}, u32[]{:S(2)}, u32[]{:S(2)}) collective-permute-start(bf16[128,512]{1,0:T(8,128)(2,1)S(1)} %get-tuple-element.61), channel_id=1, source_target_pairs={{0,2},{1,3},{2,0},{3,1},{4,6},{5,7},{6,4},{7,5},{8,10},{9,11},{10,... | collective-permute-start | bytes 393224 | tf_op jit(solution)/shard_map/ppermute | solution.py:220
  62.5 11.5 %collective-permute-start.15 = (bf16[128,512]{1,0:T(8,128)(2,1)S(1)}, bf16[128,512]{1,0:T(8,128)(2,1)S(1)}, u32[]{:S(2)}, u32[]{:S(2)}) collective-permute-start(bf16[128,512]{1,0:T(8,128)(2,1)S(1)} %get-tuple-element.61), channel_id=1, source_target_pairs={{0,6},{1,7},{2,4},{3,5},{4,2},{5,3},{6,0},{7,1},{8,14},{9,15},{10,... | collective-permute-start | bytes 393224 | tf_op jit(solution)/shard_map/ppermute | solution.py:220
  74.3 8.4 %collective-permute-start.20 = (bf16[128,512]{1,0:T(8,128)(2,1)S(1)}, bf16[128,512]{1,0:T(8,128)(2,1)S(1)}, u32[]{:S(2)}, u32[]{:S(2)}) collective-permute-start(bf16[128,512]{1,0:T(8,128)(2,1)S(1)} %get-tuple-element.64), channel_id=1, source_target_pairs={{0,8},{1,9},{2,10},{3,11},{4,12},{5,13},{6,14},{7,15},{8,16},{9,17... | collective-permute-start | bytes 393224 | tf_op jit(solution)/shard_map/ppermute | solution.py:230
  74.3 8.4 %collective-permute-start.18 = (bf16[128,512]{1,0:T(8,128)(2,1)S(1)}, bf16[128,512]{1,0:T(8,128)(2,1)S(1)}, u32[]{:S(2)}, u32[]{:S(2)}) collective-permute-start(bf16[128,512]{1,0:T(8,128)(2,1)S(1)} %get-tuple-element.63), channel_id=1, source_target_pairs={{0,10},{1,11},{2,8},{3,9},{4,14},{5,15},{6,12},{7,13},{8,18},{9,19... | collective-permute-start | bytes 393224 | tf_op jit(solution)/shard_map/ppermute | solution.py:230
  85.1 10.3 %collective-permute-start.23 = (bf16[128,512]{1,0:T(8,128)(2,1)S(1)}, bf16[128,512]{1,0:T(8,128)(2,1)S(1)}, u32[]{:S(2)}, u32[]{:S(2)}) collective-permute-start(bf16[128,512]{1,0:T(8,128)(2,1)S(1)} %get-tuple-element.66.refs_0_), channel_id=1, source_target_pairs={{0,4},{1,5},{2,6},{3,7},{4,0},{5,1},{6,2},{7,3},{8,12},{9,13},{10,... | collective-permute-start | bytes 393224 | tf_op jit(solution)/shard_map/ppermute | solution.py:220
  87.8 7.5 %collective-permute-start.24 = (bf16[128,512]{1,0:T(8,128)(2,1)S(1)}, bf16[128,512]{1,0:T(8,128)(2,1)S(1)}, u32[]{:S(2)}, u32[]{:S(2)}) collective-permute-start(bf16[128,512]{1,0:T(8,128)(2,1)S(1)} %get-tuple-element.65), channel_id=1, source_target_pairs={{0,2},{1,3},{2,0},{3,1},{4,6},{5,7},{6,4},{7,5},{8,10},{9,11},{10,... | collective-permute-start | bytes 393224 | tf_op jit(solution)/shard_map/ppermute | solution.py:220
  87.9 10.8 %collective-permute-start.22 = (bf16[128,512]{1,0:T(8,128)(2,1)S(1)}, bf16[128,512]{1,0:T(8,128)(2,1)S(1)}, u32[]{:S(2)}, u32[]{:S(2)}) collective-permute-start(bf16[128,512]{1,0:T(8,128)(2,1)S(1)} %get-tuple-element.65), channel_id=1, source_target_pairs={{0,6},{1,7},{2,4},{3,5},{4,2},{5,3},{6,0},{7,1},{8,14},{9,15},{10,... | collective-permute-start | bytes 393224 | tf_op jit(solution)/shard_map/ppermute | solution.py:220
  99.1 8.5 %collective-permute-start.27 = (bf16[128,512]{1,0:T(8,128)(2,1)S(1)}, bf16[128,512]{1,0:T(8,128)(2,1)S(1)}, u32[]{:S(2)}, u32[]{:S(2)}) collective-permute-start(bf16[128,512]{1,0:T(8,128)(2,1)S(1)} %get-tuple-element.68), channel_id=1, source_target_pairs={{0,8},{1,9},{2,10},{3,11},{4,12},{5,13},{6,14},{7,15},{8,16},{9,17... | collective-permute-start | bytes 393224 | tf_op jit(solution)/shard_map/ppermute | solution.py:230
  99.5 8.0 %collective-permute-start.25 = (bf16[128,512]{1,0:T(8,128)(2,1)S(1)}, bf16[128,512]{1,0:T(8,128)(2,1)S(1)}, u32[]{:S(2)}, u32[]{:S(2)}) collective-permute-start(bf16[128,512]{1,0:T(8,128)(2,1)S(1)} %get-tuple-element.67), channel_id=1, source_target_pairs={{0,10},{1,11},{2,8},{3,9},{4,14},{5,15},{6,12},{7,13},{8,18},{9,19... | collective-permute-start | bytes 393224 | tf_op jit(solution)/shard_map/ppermute | solution.py:230
  109.8 10.2 %collective-permute-start.30 = (bf16[128,512]{1,0:T(8,128)(2,1)S(1)}, bf16[128,512]{1,0:T(8,128)(2,1)S(1)}, u32[]{:S(2)}, u32[]{:S(2)}) collective-permute-start(bf16[128,512]{1,0:T(8,128)(2,1)S(1)} %get-tuple-element.70.refs_0_), channel_id=1, source_target_pairs={{0,4},{1,5},{2,6},{3,7},{4,0},{5,1},{6,2},{7,3},{8,12},{9,13},{10,... | collective-permute-start | bytes 393224 | tf_op jit(solution)/shard_map/ppermute | solution.py:220
  112.5 7.6 %collective-permute-start.31 = (bf16[128,512]{1,0:T(8,128)(2,1)S(1)}, bf16[128,512]{1,0:T(8,128)(2,1)S(1)}, u32[]{:S(2)}, u32[]{:S(2)}) collective-permute-start(bf16[128,512]{1,0:T(8,128)(2,1)S(1)} %get-tuple-element.69), channel_id=1, source_target_pairs={{0,2},{1,3},{2,0},{3,1},{4,6},{5,7},{6,4},{7,5},{8,10},{9,11},{10,... | collective-permute-start | bytes 393224 | tf_op jit(solution)/shard_map/ppermute | solution.py:220
  112.6 10.9 %collective-permute-start.29 = (bf16[128,512]{1,0:T(8,128)(2,1)S(1)}, bf16[128,512]{1,0:T(8,128)(2,1)S(1)}, u32[]{:S(2)}, u32[]{:S(2)}) collective-permute-start(bf16[128,512]{1,0:T(8,128)(2,1)S(1)} %get-tuple-element.69), channel_id=1, source_target_pairs={{0,6},{1,7},{2,4},{3,5},{4,2},{5,3},{6,0},{7,1},{8,14},{9,15},{10,... | collective-permute-start | bytes 393224 | tf_op jit(solution)/shard_map/ppermute | solution.py:220
  123.8 8.4 %collective-permute-start.34 = (bf16[128,512]{1,0:T(8,128)(2,1)S(1)}, bf16[128,512]{1,0:T(8,128)(2,1)S(1)}, u32[]{:S(2)}, u32[]{:S(2)}) collective-permute-start(bf16[128,512]{1,0:T(8,128)(2,1)S(1)} %get-tuple-element.72), channel_id=1, source_target_pairs={{0,8},{1,9},{2,10},{3,11},{4,12},{5,13},{6,14},{7,15},{8,16},{9,17... | collective-permute-start | bytes 393224 | tf_op jit(solution)/shard_map/ppermute | solution.py:230
  123.9 8.4 %collective-permute-start.32 = (bf16[128,512]{1,0:T(8,128)(2,1)S(1)}, bf16[128,512]{1,0:T(8,128)(2,1)S(1)}, u32[]{:S(2)}, u32[]{:S(2)}) collective-permute-start(bf16[128,512]{1,0:T(8,128)(2,1)S(1)} %get-tuple-element.71), channel_id=1, source_target_pairs={{0,10},{1,11},{2,8},{3,9},{4,14},{5,15},{6,12},{7,13},{8,18},{9,19... | collective-permute-start | bytes 393224 | tf_op jit(solution)/shard_map/ppermute | solution.py:230
  134.6 10.3 %collective-permute-start.37 = (bf16[128,512]{1,0:T(8,128)(2,1)S(1)}, bf16[128,512]{1,0:T(8,128)(2,1)S(1)}, u32[]{:S(2)}, u32[]{:S(2)}) collective-permute-start(bf16[128,512]{1,0:T(8,128)(2,1)S(1)} %get-tuple-element.74.refs_0_), channel_id=1, source_target_pairs={{0,4},{1,5},{2,6},{3,7},{4,0},{5,1},{6,2},{7,3},{8,12},{9,13},{10,... | collective-permute-start | bytes 393224 | tf_op jit(solution)/shard_map/ppermute | solution.py:220
  137.2 7.7 %collective-permute-start.38 = (bf16[128,512]{1,0:T(8,128)(2,1)S(1)}, bf16[128,512]{1,0:T(8,128)(2,1)S(1)}, u32[]{:S(2)}, u32[]{:S(2)}) collective-permute-start(bf16[128,512]{1,0:T(8,128)(2,1)S(1)} %get-tuple-element.73), channel_id=1, source_target_pairs={{0,2},{1,3},{2,0},{3,1},{4,6},{5,7},{6,4},{7,5},{8,10},{9,11},{10,... | collective-permute-start | bytes 393224 | tf_op jit(solution)/shard_map/ppermute | solution.py:220
  137.3 10.9 %collective-permute-start.36 = (bf16[128,512]{1,0:T(8,128)(2,1)S(1)}, bf16[128,512]{1,0:T(8,128)(2,1)S(1)}, u32[]{:S(2)}, u32[]{:S(2)}) collective-permute-start(bf16[128,512]{1,0:T(8,128)(2,1)S(1)} %get-tuple-element.73), channel_id=1, source_target_pairs={{0,6},{1,7},{2,4},{3,5},{4,2},{5,3},{6,0},{7,1},{8,14},{9,15},{10,... | collective-permute-start | bytes 393224 | tf_op jit(solution)/shard_map/ppermute | solution.py:220
  148.5 8.4 %collective-permute-start.41 = (bf16[128,512]{1,0:T(8,128)(2,1)S(1)}, bf16[128,512]{1,0:T(8,128)(2,1)S(1)}, u32[]{:S(2)}, u32[]{:S(2)}) collective-permute-start(bf16[128,512]{1,0:T(8,128)(2,1)S(1)} %get-tuple-element.76), channel_id=1, source_target_pairs={{0,8},{1,9},{2,10},{3,11},{4,12},{5,13},{6,14},{7,15},{8,16},{9,17... | collective-permute-start | bytes 393224 | tf_op jit(solution)/shard_map/ppermute | solution.py:230
  148.6 8.4 %collective-permute-start.39 = (bf16[128,512]{1,0:T(8,128)(2,1)S(1)}, bf16[128,512]{1,0:T(8,128)(2,1)S(1)}, u32[]{:S(2)}, u32[]{:S(2)}) collective-permute-start(bf16[128,512]{1,0:T(8,128)(2,1)S(1)} %get-tuple-element.75), channel_id=1, source_target_pairs={{0,10},{1,11},{2,8},{3,9},{4,14},{5,15},{6,12},{7,13},{8,18},{9,19... | collective-permute-start | bytes 393224 | tf_op jit(solution)/shard_map/ppermute | solution.py:230
  159.2 10.2 %collective-permute-start.44 = (bf16[128,512]{1,0:T(8,128)(2,1)S(1)}, bf16[128,512]{1,0:T(8,128)(2,1)S(1)}, u32[]{:S(2)}, u32[]{:S(2)}) collective-permute-start(bf16[128,512]{1,0:T(8,128)(2,1)S(1)} %get-tuple-element.78.refs_0_), channel_id=1, source_target_pairs={{0,4},{1,5},{2,6},{3,7},{4,0},{5,1},{6,2},{7,3},{8,12},{9,13},{10,... | collective-permute-start | bytes 393224 | tf_op jit(solution)/shard_map/ppermute | solution.py:220
  161.9 7.6 %collective-permute-start.45 = (bf16[128,512]{1,0:T(8,128)(2,1)S(1)}, bf16[128,512]{1,0:T(8,128)(2,1)S(1)}, u32[]{:S(2)}, u32[]{:S(2)}) collective-permute-start(bf16[128,512]{1,0:T(8,128)(2,1)S(1)} %get-tuple-element.77), channel_id=1, source_target_pairs={{0,2},{1,3},{2,0},{3,1},{4,6},{5,7},{6,4},{7,5},{8,10},{9,11},{10,... | collective-permute-start | bytes 393224 | tf_op jit(solution)/shard_map/ppermute | solution.py:220
  162.0 10.9 %collective-permute-start.43 = (bf16[128,512]{1,0:T(8,128)(2,1)S(1)}, bf16[128,512]{1,0:T(8,128)(2,1)S(1)}, u32[]{:S(2)}, u32[]{:S(2)}) collective-permute-start(bf16[128,512]{1,0:T(8,128)(2,1)S(1)} %get-tuple-element.77), channel_id=1, source_target_pairs={{0,6},{1,7},{2,4},{3,5},{4,2},{5,3},{6,0},{7,1},{8,14},{9,15},{10,... | collective-permute-start | bytes 393224 | tf_op jit(solution)/shard_map/ppermute | solution.py:220
  (18 other events, 43.3 us)

commit v2 on v1

--- a/solution.py
+++ b/solution.py
@@ -10,7 +10,6 @@
 MIB = 1024 * 1024
 PLACE_VMEM = 46 * MIB
 LAYER_VMEM = 16 * MIB
-WEIGHT_COPIES = 4
 WHOLE = pl.BlockSpec(memory_space=pltpu.VMEM)
 TABLE = pl.BlockSpec(memory_space=pltpu.SMEM)
 
@@ -51,9 +50,8 @@
             place(pair)
 
 
-def placed(layer, weights, biases, tile_index, columns, slots_of, order):
+def placed(layer, weights, biases, tile_index, columns, slots_of, order, copies):
     _, slots, tile, width = weights.shape
-    copies = min(WEIGHT_COPIES, slots // 2)
     away = pl.BlockSpec(memory_space=pltpu.HBM)
     return pl.pallas_call(
         functools.partial(place_kernel, layer, order),
@@ -210,11 +208,11 @@
     columns = jnp.stack([even_columns, odd_columns])
     spot = jnp.arange(local, dtype=jnp.int32)
     slots_of = spot % deep * group + ((spot // deep) ^ near)
-    first_of = [(2 * pair) % deep * group if deep > 1 else 2 * pair for pair in range(local // 2)]
-    order = sorted(range(local // 2), key=lambda pair: (first_of[pair], pair))
+    copies = max(1, deep // 2)
+    order = sorted(range(local // 2), key=lambda pair: (2 * pair % deep, pair))
     place = jnp.broadcast_to(jnp.stack([segment, near]).astype(jnp.int32)[:, None, None], (2, 8, max(batch, 4 * tile)))
     columns, slots_of, place, first = lax.optimization_barrier((columns, slots_of, place, segment == 0))
-    layers = [placed(index, weights, biases, tile_index, columns, slots_of, order) for index in range(2)]
+    layers = [placed(index, weights, biases, tile_index, columns, slots_of, order, copies) for index in range(2)]
 
     def along(value, flip):
         return lax.ppermute(value, "blk", [(i, i ^ flip) for i in range(devices)])

time: 179 us -> 179 us (level)
  no operation moved by 1% of the time
where the time goes in v2:
time: 179 us
  waiting for transfers between devices  89.5 us (50%)
  starting transfers between devices  65.5 us (37%)
  Pallas kernels  22 us (12%)
    ppermute x35, waiting for transfers between devices, along(): return lax.ppermute(value, 'blk', [(i, i ^ flip) for i in range(devices)])  64.9 us
    ppermute x35, starting transfers between devices, along(): return lax.ppermute(value, 'blk', [(i, i ^ flip) for i in range(devices)])  39.3 us
    ppermute x12, starting transfers between devices, passed(): lax.ppermute(part, ('segment', 'blk'), [(s * devices + i, (s + 1) % segme...  26.2 us
    ppermute x12, waiting for transfers between devices, passed(): lax.ppermute(part, ('segment', 'blk'), [(s * devices + i, (s + 1) % segme...  24.6 us
    pallas_call x13, Pallas kernels, layer(): pl.pallas_call(early_kernel, in_specs=[WHOLE] * (len(early) + 2), out_spe...  8.08 us
    pallas_call x2, Pallas kernels, placed(): pl.pallas_call(functools.partial(place_kernel, layer, order), in_specs=[T...  7.7 us
    pallas_call x14, Pallas kernels, layer(): pl.pallas_call(functools.partial(layer_kernel, len(pieces), outs, depth,...  4.81 us
  transfers between devices with their start and end apart: 47, of which 28 were waited for; matrix products, arithmetic and copies ran while one was open for 0% of the time, Pallas kernels for 9%

profile of v2, /device:TPU:0, one launch (start us, length us, event | category | flops | bytes accessed | tf_op | source)
XLA Modules:
  0.0 179.1 jit_solution(14871432728537036218)
XLA Ops:
  2.1 3.6 %place_tiles.2 = (bf16[8,2048,128]{2,1,0:T(8,128)(2,1)S(1)}, f32[1,1024]{1,0:T(1,128)S(1)}) custom-call(s32[2,32]{1,0:T(2,128)S(1)} %pad_add_fusion.column_ref, s32[16]{0:T(128)S(1)} %fusion.3.slot_ref, f32[2,16,64]{2,1,0:T(8,128)S(1)} %copy-done.1, s32[2,16,32]{2,1,0:T(8,128)S(1)} %copy-done.2, bf16[2,16,64,2048]{3,2,1,0:T(8,128)(2,1)} %weights_ref.3), custom_call_target="tpu_custom_call" | custom-call | tf_op jit(solution)/shard_map/place_tiles/pallas_call | solution.py:56
  6.7 3.7 %collective-permute-start.2 = (bf16[128,512]{1,0:T(8,128)(2,1)S(1)}, bf16[128,512]{1,0:T(8,128)(2,1)S(1)}, u32[]{:S(2)}, u32[]{:S(2)}) collective-permute-start(bf16[128,512]{1,0:T(8,128)(2,1)S(1)} %get-tuple-element.53.refs_0_), channel_id=1, source_target_pairs={{0,4},{1,5},{2,6},{3,7},{4,0},{5,1},{6,2},{7,3},{8,12},{9,13},{10,... | collective-permute-start | bytes 393224 | tf_op jit(solution)/shard_map/ppermute | solution.py:218
  11.9 4.1 %place_tiles.3 = (bf16[8,2048,128]{2,1,0:T(8,128)(2,1)S(1)}, f32[1,1024]{1,0:T(1,128)S(1)}) custom-call(s32[2,32]{1,0:T(2,128)S(1)} %pad_add_fusion.column_ref, s32[16]{0:T(128)S(1)} %fusion.3.slot_ref, f32[2,16,64]{2,1,0:T(8,128)S(1)} %copy-done.1, s32[2,16,32]{2,1,0:T(8,128)S(1)} %copy-done.2, bf16[2,16,64,2048]{3,2,1,0:T(8,128)(2,1)} %weights_ref.3), custom_call_target="tpu_custom_call" | custom-call | tf_op jit(solution)/shard_map/place_tiles/pallas_call | solution.py:56
  18.3 3.1 %collective-permute-done.1.refs_0_ = bf16[128,512]{1,0:T(8,128)(2,1)S(1)} collective-permute-done((bf16[128,512]{1,0:T(8,128)(2,1)S(1)}, bf16[128,512]{1,0:T(8,128)(2,1)S(1)}, u32[]{:S(2)}, u32[]{:S(2)}) %collective-permute-start.1) | collective-permute-done | bytes 131104 | tf_op jit(solution)/shard_map/ppermute | solution.py:218
  23.2 3.3 %collective-permute-start.4 = (bf16[128,512]{1,0:T(8,128)(2,1)S(1)}, bf16[128,512]{1,0:T(8,128)(2,1)S(1)}, u32[]{:S(2)}, u32[]{:S(2)}) collective-permute-start(bf16[128,512]{1,0:T(8,128)(2,1)S(1)} %get-tuple-element.55), channel_id=1, source_target_pairs={{0,10},{1,11},{2,8},{3,9},{4,14},{5,15},{6,12},{7,13},{8,18},{9,19... | collective-permute-start | bytes 393224 | tf_op jit(solution)/shard_map/ppermute | solution.py:228
  26.6 3.9 %collective-permute-done.6 = bf16[128,512]{1,0:T(8,128)(2,1)S(1)} collective-permute-done((bf16[128,512]{1,0:T(8,128)(2,1)S(1)}, bf16[128,512]{1,0:T(8,128)(2,1)S(1)}, u32[]{:S(2)}, u32[]{:S(2)}) %collective-permute-start.6) | collective-permute-done | bytes 131104 | tf_op jit(solution)/shard_map/ppermute | solution.py:228
  32.9 4.7 %collective-permute-start.9 = (bf16[128,512]{1,0:T(8,128)(2,1)S(1)}, bf16[128,512]{1,0:T(8,128)(2,1)S(1)}, u32[]{:S(2)}, u32[]{:S(2)}) collective-permute-start(bf16[128,512]{1,0:T(8,128)(2,1)S(1)} %get-tuple-element.58.refs_0_), channel_id=1, source_target_pairs={{0,4},{1,5},{2,6},{3,7},{4,0},{5,1},{6,2},{7,3},{8,12},{9,13},{10,... | collective-permute-start | bytes 393224 | tf_op jit(solution)/shard_map/ppermute | solution.py:218
  39.2 6.2 %collective-permute-done.9.refs_1_ = bf16[128,512]{1,0:T(8,128)(2,1)S(1)} collective-permute-done((bf16[128,512]{1,0:T(8,128)(2,1)S(1)}, bf16[128,512]{1,0:T(8,128)(2,1)S(1)}, u32[]{:S(2)}, u32[]{:S(2)}) %collective-permute-start.9) | collective-permute-done | bytes 131104 | tf_op jit(solution)/shard_map/ppermute | solution.py:218
  45.3 2.9 %collective-permute-done.10.refs_2_ = bf16[128,512]{1,0:T(8,128)(2,1)S(1)} collective-permute-done((bf16[128,512]{1,0:T(8,128)(2,1)S(1)}, bf16[128,512]{1,0:T(8,128)(2,1)S(1)}, u32[]{:S(2)}, u32[]{:S(2)}) %collective-permute-start.10) | collective-permute-done | bytes 131104 | tf_op jit(solution)/shard_map/ppermute | solution.py:218
  49.9 3.4 %collective-permute-start.11 = (bf16[128,512]{1,0:T(8,128)(2,1)S(1)}, bf16[128,512]{1,0:T(8,128)(2,1)S(1)}, u32[]{:S(2)}, u32[]{:S(2)}) collective-permute-start(bf16[128,512]{1,0:T(8,128)(2,1)S(1)} %get-tuple-element.59), channel_id=1, source_target_pairs={{0,10},{1,11},{2,8},{3,9},{4,14},{5,15},{6,12},{7,13},{8,18},{9,19... | collective-permute-start | bytes 393224 | tf_op jit(solution)/shard_map/ppermute | solution.py:228
  53.4 4.5 %collective-permute-done.13 = bf16[128,512]{1,0:T(8,128)(2,1)S(1)} collective-permute-done((bf16[128,512]{1,0:T(8,128)(2,1)S(1)}, bf16[128,512]{1,0:T(8,128)(2,1)S(1)}, u32[]{:S(2)}, u32[]{:S(2)}) %collective-permute-start.13) | collective-permute-done | bytes 131104 | tf_op jit(solution)/shard_map/ppermute | solution.py:228
  64.7 5.9 %collective-permute-done.16.refs_1_ = bf16[128,512]{1,0:T(8,128)(2,1)S(1)} collective-permute-done((bf16[128,512]{1,0:T(8,128)(2,1)S(1)}, bf16[128,512]{1,0:T(8,128)(2,1)S(1)}, u32[]{:S(2)}, u32[]{:S(2)}) %collective-permute-start.16) | collective-permute-done | bytes 131104 | tf_op jit(solution)/shard_map/ppermute | solution.py:218
  71.2 2.7 %collective-permute-done.15.refs_0_ = bf16[128,512]{1,0:T(8,128)(2,1)S(1)} collective-permute-done((bf16[128,512]{1,0:T(8,128)(2,1)S(1)}, bf16[128,512]{1,0:T(8,128)(2,1)S(1)}, u32[]{:S(2)}, u32[]{:S(2)}) %collective-permute-start.15) | collective-permute-done | bytes 131104 | tf_op jit(solution)/shard_map/ppermute | solution.py:218
  74.3 4.3 %collective-permute-start.18 = (bf16[128,512]{1,0:T(8,128)(2,1)S(1)}, bf16[128,512]{1,0:T(8,128)(2,1)S(1)}, u32[]{:S(2)}, u32[]{:S(2)}) collective-permute-start(bf16[128,512]{1,0:T(8,128)(2,1)S(1)} %get-tuple-element.63), channel_id=1, source_target_pairs={{0,10},{1,11},{2,8},{3,9},{4,14},{5,15},{6,12},{7,13},{8,18},{9,19... | collective-permute-start | bytes 393224 | tf_op jit(solution)/shard_map/ppermute | solution.py:228
  78.7 4.0 %collective-permute-done.20 = bf16[128,512]{1,0:T(8,128)(2,1)S(1)} collective-permute-done((bf16[128,512]{1,0:T(8,128)(2,1)S(1)}, bf16[128,512]{1,0:T(8,128)(2,1)S(1)}, u32[]{:S(2)}, u32[]{:S(2)}) %collective-permute-start.20) | collective-permute-done | bytes 131104 | tf_op jit(solution)/shard_map/ppermute | solution.py:228
  85.1 2.8 %collective-permute-start.23 = (bf16[128,512]{1,0:T(8,128)(2,1)S(1)}, bf16[128,512]{1,0:T(8,128)(2,1)S(1)}, u32[]{:S(2)}, u32[]{:S(2)}) collective-permute-start(bf16[128,512]{1,0:T(8,128)(2,1)S(1)} %get-tuple-element.66.refs_0_), channel_id=1, source_target_pairs={{0,4},{1,5},{2,6},{3,7},{4,0},{5,1},{6,2},{7,3},{8,12},{9,13},{10,... | collective-permute-start | bytes 393224 | tf_op jit(solution)/shard_map/ppermute | solution.py:218
  89.5 5.8 %collective-permute-done.23.refs_1_ = bf16[128,512]{1,0:T(8,128)(2,1)S(1)} collective-permute-done((bf16[128,512]{1,0:T(8,128)(2,1)S(1)}, bf16[128,512]{1,0:T(8,128)(2,1)S(1)}, u32[]{:S(2)}, u32[]{:S(2)}) %collective-permute-start.23) | collective-permute-done | bytes 131104 | tf_op jit(solution)/shard_map/ppermute | solution.py:218
  96.0 2.7 %collective-permute-done.22.refs_0_ = bf16[128,512]{1,0:T(8,128)(2,1)S(1)} collective-permute-done((bf16[128,512]{1,0:T(8,128)(2,1)S(1)}, bf16[128,512]{1,0:T(8,128)(2,1)S(1)}, u32[]{:S(2)}, u32[]{:S(2)}) %collective-permute-start.22) | collective-permute-done | bytes 131104 | tf_op jit(solution)/shard_map/ppermute | solution.py:218
  99.5 3.9 %collective-permute-start.25 = (bf16[128,512]{1,0:T(8,128)(2,1)S(1)}, bf16[128,512]{1,0:T(8,128)(2,1)S(1)}, u32[]{:S(2)}, u32[]{:S(2)}) collective-permute-start(bf16[128,512]{1,0:T(8,128)(2,1)S(1)} %get-tuple-element.67), channel_id=1, source_target_pairs={{0,10},{1,11},{2,8},{3,9},{4,14},{5,15},{6,12},{7,13},{8,18},{9,19... | collective-permute-start | bytes 393224 | tf_op jit(solution)/shard_map/ppermute | solution.py:228
  103.4 4.1 %collective-permute-done.27.refs_0_.refs_4_ = bf16[128,512]{1,0:T(8,128)(2,1)S(1)} collective-permute-done((bf16[128,512]{1,0:T(8,128)(2,1)S(1)}, bf16[128,512]{1,0:T(8,128)(2,1)S(1)}, u32[]{:S(2)}, u32[]{:S(2)}) %collective-permute-start.27) | collective-permute-done | bytes 131104 | tf_op jit(solution)/shard_map/ppermute | solution.py:228
  114.3 5.8 %collective-permute-done.30.refs_1_ = bf16[128,512]{1,0:T(8,128)(2,1)S(1)} collective-permute-done((bf16[128,512]{1,0:T(8,128)(2,1)S(1)}, bf16[128,512]{1,0:T(8,128)(2,1)S(1)}, u32[]{:S(2)}, u32[]{:S(2)}) %collective-permute-start.30) | collective-permute-done | bytes 131104 | tf_op jit(solution)/shard_map/ppermute | solution.py:218
  120.7 2.8 %collective-permute-done.29.refs_0_ = bf16[128,512]{1,0:T(8,128)(2,1)S(1)} collective-permute-done((bf16[128,512]{1,0:T(8,128)(2,1)S(1)}, bf16[128,512]{1,0:T(8,128)(2,1)S(1)}, u32[]{:S(2)}, u32[]{:S(2)}) %collective-permute-start.29) | collective-permute-done | bytes 131104 | tf_op jit(solution)/shard_map/ppermute | solution.py:218
  123.9 4.2 %collective-permute-start.32 = (bf16[128,512]{1,0:T(8,128)(2,1)S(1)}, bf16[128,512]{1,0:T(8,128)(2,1)S(1)}, u32[]{:S(2)}, u32[]{:S(2)}) collective-permute-start(bf16[128,512]{1,0:T(8,128)(2,1)S(1)} %get-tuple-element.71), channel_id=1, source_target_pairs={{0,10},{1,11},{2,8},{3,9},{4,14},{5,15},{6,12},{7,13},{8,18},{9,19... | collective-permute-start | bytes 393224 | tf_op jit(solution)/shard_map/ppermute | solution.py:228
  128.1 4.1 %collective-permute-done.34.refs_0_.refs_4_ = bf16[128,512]{1,0:T(8,128)(2,1)S(1)} collective-permute-done((bf16[128,512]{1,0:T(8,128)(2,1)S(1)}, bf16[128,512]{1,0:T(8,128)(2,1)S(1)}, u32[]{:S(2)}, u32[]{:S(2)}) %collective-permute-start.34) | collective-permute-done | bytes 131104 | tf_op jit(solution)/shard_map/ppermute | solution.py:228
  134.6 2.7 %collective-permute-start.37 = (bf16[128,512]{1,0:T(8,128)(2,1)S(1)}, bf16[128,512]{1,0:T(8,128)(2,1)S(1)}, u32[]{:S(2)}, u32[]{:S(2)}) collective-permute-start(bf16[128,512]{1,0:T(8,128)(2,1)S(1)} %get-tuple-element.74.refs_0_), channel_id=1, source_target_pairs={{0,4},{1,5},{2,6},{3,7},{4,0},{5,1},{6,2},{7,3},{8,12},{9,13},{10,... | collective-permute-start | bytes 393224 | tf_op jit(solution)/shard_map/ppermute | solution.py:218
  139.0 5.9 %collective-permute-done.37.refs_1_ = bf16[128,512]{1,0:T(8,128)(2,1)S(1)} collective-permute-done((bf16[128,512]{1,0:T(8,128)(2,1)S(1)}, bf16[128,512]{1,0:T(8,128)(2,1)S(1)}, u32[]{:S(2)}, u32[]{:S(2)}) %collective-permute-start.37) | collective-permute-done | bytes 131104 | tf_op jit(solution)/shard_map/ppermute | solution.py:218
  148.6 4.3 %collective-permute-start.39 = (bf16[128,512]{1,0:T(8,128)(2,1)S(1)}, bf16[128,512]{1,0:T(8,128)(2,1)S(1)}, u32[]{:S(2)}, u32[]{:S(2)}) collective-permute-start(bf16[128,512]{1,0:T(8,128)(2,1)S(1)} %get-tuple-element.75), channel_id=1, source_target_pairs={{0,10},{1,11},{2,8},{3,9},{4,14},{5,15},{6,12},{7,13},{8,18},{9,19... | collective-permute-start | bytes 393224 | tf_op jit(solution)/shard_map/ppermute | solution.py:228
  152.9 4.1 %collective-permute-done.41.refs_0_.refs_4_ = bf16[128,512]{1,0:T(8,128)(2,1)S(1)} collective-permute-done((bf16[128,512]{1,0:T(8,128)(2,1)S(1)}, bf16[128,512]{1,0:T(8,128)(2,1)S(1)}, u32[]{:S(2)}, u32[]{:S(2)}) %collective-permute-start.41) | collective-permute-done | bytes 131104 | tf_op jit(solution)/shard_map/ppermute | solution.py:228
  159.2 2.7 %collective-permute-start.44 = (bf16[128,512]{1,0:T(8,128)(2,1)S(1)}, bf16[128,512]{1,0:T(8,128)(2,1)S(1)}, u32[]{:S(2)}, u32[]{:S(2)}) collective-permute-start(bf16[128,512]{1,0:T(8,128)(2,1)S(1)} %get-tuple-element.78.refs_0_), channel_id=1, source_target_pairs={{0,4},{1,5},{2,6},{3,7},{4,0},{5,1},{6,2},{7,3},{8,12},{9,13},{10,... | collective-permute-start | bytes 393224 | tf_op jit(solution)/shard_map/ppermute | solution.py:218
  163.7 5.8 %collective-permute-done.44.refs_1_ = bf16[128,512]{1,0:T(8,128)(2,1)S(1)} collective-permute-done((bf16[128,512]{1,0:T(8,128)(2,1)S(1)}, bf16[128,512]{1,0:T(8,128)(2,1)S(1)}, u32[]{:S(2)}, u32[]{:S(2)}) %collective-permute-start.44) | collective-permute-done | bytes 131104 | tf_op jit(solution)/shard_map/ppermute | solution.py:218
  170.1 2.8 %collective-permute-done.43.refs_0_ = bf16[128,512]{1,0:T(8,128)(2,1)S(1)} collective-permute-done((bf16[128,512]{1,0:T(8,128)(2,1)S(1)}, bf16[128,512]{1,0:T(8,128)(2,1)S(1)}, u32[]{:S(2)}, u32[]{:S(2)}) %collective-permute-start.43) | collective-permute-done | bytes 131104 | tf_op jit(solution)/shard_map/ppermute | solution.py:218
  175.1 3.1 %collective-permute-done.46.refs_2_ = bf16[128,512]{1,0:T(8,128)(2,1)S(1)} collective-permute-done((bf16[128,512]{1,0:T(8,128)(2,1)S(1)}, bf16[128,512]{1,0:T(8,128)(2,1)S(1)}, u32[]{:S(2)}, u32[]{:S(2)}) %collective-permute-start.46) | collective-permute-done | bytes 131104 | tf_op jit(solution)/shard_map/ppermute | solution.py:218
  (110 shorter events, 51.1 us)
Async XLA Ops:
  6.7 10.9 %collective-permute-start.2 = (bf16[128,512]{1,0:T(8,128)(2,1)S(1)}, bf16[128,512]{1,0:T(8,128)(2,1)S(1)}, u32[]{:S(2)}, u32[]{:S(2)}) collective-permute-start(bf16[128,512]{1,0:T(8,128)(2,1)S(1)} %get-tuple-element.53.refs_0_), channel_id=1, source_target_pairs={{0,4},{1,5},{2,6},{3,7},{4,0},{5,1},{6,2},{7,3},{8,12},{9,13},{10,... | collective-permute-start | bytes 393224 | tf_op jit(solution)/shard_map/ppermute | solution.py:218
  11.9 9.4 %collective-permute-start.1 = (bf16[128,512]{1,0:T(8,128)(2,1)S(1)}, bf16[128,512]{1,0:T(8,128)(2,1)S(1)}, u32[]{:S(2)}, u32[]{:S(2)}) collective-permute-start(bf16[128,512]{1,0:T(8,128)(2,1)S(1)} %get-tuple-element.51), channel_id=1, source_target_pairs={{0,6},{1,7},{2,4},{3,5},{4,2},{5,3},{6,0},{7,1},{8,14},{9,15},{10,... | collective-permute-start | bytes 393224 | tf_op jit(solution)/shard_map/ppermute | solution.py:218
  21.7 8.8 %collective-permute-start.6 = (bf16[128,512]{1,0:T(8,128)(2,1)S(1)}, bf16[128,512]{1,0:T(8,128)(2,1)S(1)}, u32[]{:S(2)}, u32[]{:S(2)}) collective-permute-start(bf16[128,512]{1,0:T(8,128)(2,1)S(1)} %get-tuple-element.56), channel_id=1, source_target_pairs={{0,8},{1,9},{2,10},{3,11},{4,12},{5,13},{6,14},{7,15},{8,16},{9,17... | collective-permute-start | bytes 393224 | tf_op jit(solution)/shard_map/ppermute | solution.py:228
  23.2 7.3 %collective-permute-start.4 = (bf16[128,512]{1,0:T(8,128)(2,1)S(1)}, bf16[128,512]{1,0:T(8,128)(2,1)S(1)}, u32[]{:S(2)}, u32[]{:S(2)}) collective-permute-start(bf16[128,512]{1,0:T(8,128)(2,1)S(1)} %get-tuple-element.55), channel_id=1, source_target_pairs={{0,10},{1,11},{2,8},{3,9},{4,14},{5,15},{6,12},{7,13},{8,18},{9,19... | collective-permute-start | bytes 393224 | tf_op jit(solution)/shard_map/ppermute | solution.py:228
  32.9 12.4 %collective-permute-start.9 = (bf16[128,512]{1,0:T(8,128)(2,1)S(1)}, bf16[128,512]{1,0:T(8,128)(2,1)S(1)}, u32[]{:S(2)}, u32[]{:S(2)}) collective-permute-start(bf16[128,512]{1,0:T(8,128)(2,1)S(1)} %get-tuple-element.58.refs_0_), channel_id=1, source_target_pairs={{0,4},{1,5},{2,6},{3,7},{4,0},{5,1},{6,2},{7,3},{8,12},{9,13},{10,... | collective-permute-start | bytes 393224 | tf_op jit(solution)/shard_map/ppermute | solution.py:218
  37.6 10.6 %collective-permute-start.10 = (bf16[128,512]{1,0:T(8,128)(2,1)S(1)}, bf16[128,512]{1,0:T(8,128)(2,1)S(1)}, u32[]{:S(2)}, u32[]{:S(2)}) collective-permute-start(bf16[128,512]{1,0:T(8,128)(2,1)S(1)} %get-tuple-element.57), channel_id=1, source_target_pairs={{0,2},{1,3},{2,0},{3,1},{4,6},{5,7},{6,4},{7,5},{8,10},{9,11},{10,... | collective-permute-start | bytes 393224 | tf_op jit(solution)/shard_map/ppermute | solution.py:218
  37.6 11.3 %collective-permute-start.8 = (bf16[128,512]{1,0:T(8,128)(2,1)S(1)}, bf16[128,512]{1,0:T(8,128)(2,1)S(1)}, u32[]{:S(2)}, u32[]{:S(2)}) collective-permute-start(bf16[128,512]{1,0:T(8,128)(2,1)S(1)} %get-tuple-element.57), channel_id=1, source_target_pairs={{0,6},{1,7},{2,4},{3,5},{4,2},{5,3},{6,0},{7,1},{8,14},{9,15},{10,... | collective-permute-start | bytes 393224 | tf_op jit(solution)/shard_map/ppermute | solution.py:218
  49.2 8.6 %collective-permute-start.13 = (bf16[128,512]{1,0:T(8,128)(2,1)S(1)}, bf16[128,512]{1,0:T(8,128)(2,1)S(1)}, u32[]{:S(2)}, u32[]{:S(2)}) collective-permute-start(bf16[128,512]{1,0:T(8,128)(2,1)S(1)} %get-tuple-element.60), channel_id=1, source_target_pairs={{0,8},{1,9},{2,10},{3,11},{4,12},{5,13},{6,14},{7,15},{8,16},{9,17... | collective-permute-start | bytes 393224 | tf_op jit(solution)/shard_map/ppermute | solution.py:228
  49.9 8.0 %collective-permute-start.11 = (bf16[128,512]{1,0:T(8,128)(2,1)S(1)}, bf16[128,512]{1,0:T(8,128)(2,1)S(1)}, u32[]{:S(2)}, u32[]{:S(2)}) collective-permute-start(bf16[128,512]{1,0:T(8,128)(2,1)S(1)} %get-tuple-element.59), channel_id=1, source_target_pairs={{0,10},{1,11},{2,8},{3,9},{4,14},{5,15},{6,12},{7,13},{8,18},{9,19... | collective-permute-start | bytes 393224 | tf_op jit(solution)/shard_map/ppermute | solution.py:228
  60.3 10.3 %collective-permute-start.16 = (bf16[128,512]{1,0:T(8,128)(2,1)S(1)}, bf16[128,512]{1,0:T(8,128)(2,1)S(1)}, u32[]{:S(2)}, u32[]{:S(2)}) collective-permute-start(bf16[128,512]{1,0:T(8,128)(2,1)S(1)} %get-tuple-element.62.refs_0_), channel_id=1, source_target_pairs={{0,4},{1,5},{2,6},{3,7},{4,0},{5,1},{6,2},{7,3},{8,12},{9,13},{10,... | collective-permute-start | bytes 393224 | tf_op jit(solution)/shard_map/ppermute | solution.py:218
  61.3 9.3 %collective-permute-start.17 = (bf16[128,512]{1,0:T(8,128)(2,1)S(1)}, bf16[128,512]{1,0:T(8,128)(2,1)S(1)}, u32[]{:S(2)}, u32[]{:S(2)}) collective-permute-start(bf16[128,512]{1,0:T(8,128)(2,1)S(1)} %get-tuple-element.61), channel_id=1, source_target_pairs={{0,2},{1,3},{2,0},{3,1},{4,6},{5,7},{6,4},{7,5},{8,10},{9,11},{10,... | collective-permute-start | bytes 393224 | tf_op jit(solution)/shard_map/ppermute | solution.py:218
  62.5 11.5 %collective-permute-start.15 = (bf16[128,512]{1,0:T(8,128)(2,1)S(1)}, bf16[128,512]{1,0:T(8,128)(2,1)S(1)}, u32[]{:S(2)}, u32[]{:S(2)}) collective-permute-start(bf16[128,512]{1,0:T(8,128)(2,1)S(1)} %get-tuple-element.61), channel_id=1, source_target_pairs={{0,6},{1,7},{2,4},{3,5},{4,2},{5,3},{6,0},{7,1},{8,14},{9,15},{10,... | collective-permute-start | bytes 393224 | tf_op jit(solution)/shard_map/ppermute | solution.py:218
  74.3 8.4 %collective-permute-start.20 = (bf16[128,512]{1,0:T(8,128)(2,1)S(1)}, bf16[128,512]{1,0:T(8,128)(2,1)S(1)}, u32[]{:S(2)}, u32[]{:S(2)}) collective-permute-start(bf16[128,512]{1,0:T(8,128)(2,1)S(1)} %get-tuple-element.64), channel_id=1, source_target_pairs={{0,8},{1,9},{2,10},{3,11},{4,12},{5,13},{6,14},{7,15},{8,16},{9,17... | collective-permute-start | bytes 393224 | tf_op jit(solution)/shard_map/ppermute | solution.py:228
  74.3 8.4 %collective-permute-start.18 = (bf16[128,512]{1,0:T(8,128)(2,1)S(1)}, bf16[128,512]{1,0:T(8,128)(2,1)S(1)}, u32[]{:S(2)}, u32[]{:S(2)}) collective-permute-start(bf16[128,512]{1,0:T(8,128)(2,1)S(1)} %get-tuple-element.63), channel_id=1, source_target_pairs={{0,10},{1,11},{2,8},{3,9},{4,14},{5,15},{6,12},{7,13},{8,18},{9,19... | collective-permute-start | bytes 393224 | tf_op jit(solution)/shard_map/ppermute | solution.py:228
  85.1 10.3 %collective-permute-start.23 = (bf16[128,512]{1,0:T(8,128)(2,1)S(1)}, bf16[128,512]{1,0:T(8,128)(2,1)S(1)}, u32[]{:S(2)}, u32[]{:S(2)}) collective-permute-start(bf16[128,512]{1,0:T(8,128)(2,1)S(1)} %get-tuple-element.66.refs_0_), channel_id=1, source_target_pairs={{0,4},{1,5},{2,6},{3,7},{4,0},{5,1},{6,2},{7,3},{8,12},{9,13},{10,... | collective-permute-start | bytes 393224 | tf_op jit(solution)/shard_map/ppermute | solution.py:218
  87.8 7.5 %collective-permute-start.24 = (bf16[128,512]{1,0:T(8,128)(2,1)S(1)}, bf16[128,512]{1,0:T(8,128)(2,1)S(1)}, u32[]{:S(2)}, u32[]{:S(2)}) collective-permute-start(bf16[128,512]{1,0:T(8,128)(2,1)S(1)} %get-tuple-element.65), channel_id=1, source_target_pairs={{0,2},{1,3},{2,0},{3,1},{4,6},{5,7},{6,4},{7,5},{8,10},{9,11},{10,... | collective-permute-start | bytes 393224 | tf_op jit(solution)/shard_map/ppermute | solution.py:218
  87.9 10.8 %collective-permute-start.22 = (bf16[128,512]{1,0:T(8,128)(2,1)S(1)}, bf16[128,512]{1,0:T(8,128)(2,1)S(1)}, u32[]{:S(2)}, u32[]{:S(2)}) collective-permute-start(bf16[128,512]{1,0:T(8,128)(2,1)S(1)} %get-tuple-element.65), channel_id=1, source_target_pairs={{0,6},{1,7},{2,4},{3,5},{4,2},{5,3},{6,0},{7,1},{8,14},{9,15},{10,... | collective-permute-start | bytes 393224 | tf_op jit(solution)/shard_map/ppermute | solution.py:218
  99.1 8.5 %collective-permute-start.27 = (bf16[128,512]{1,0:T(8,128)(2,1)S(1)}, bf16[128,512]{1,0:T(8,128)(2,1)S(1)}, u32[]{:S(2)}, u32[]{:S(2)}) collective-permute-start(bf16[128,512]{1,0:T(8,128)(2,1)S(1)} %get-tuple-element.68), channel_id=1, source_target_pairs={{0,8},{1,9},{2,10},{3,11},{4,12},{5,13},{6,14},{7,15},{8,16},{9,17... | collective-permute-start | bytes 393224 | tf_op jit(solution)/shard_map/ppermute | solution.py:228
  99.5 8.0 %collective-permute-start.25 = (bf16[128,512]{1,0:T(8,128)(2,1)S(1)}, bf16[128,512]{1,0:T(8,128)(2,1)S(1)}, u32[]{:S(2)}, u32[]{:S(2)}) collective-permute-start(bf16[128,512]{1,0:T(8,128)(2,1)S(1)} %get-tuple-element.67), channel_id=1, source_target_pairs={{0,10},{1,11},{2,8},{3,9},{4,14},{5,15},{6,12},{7,13},{8,18},{9,19... | collective-permute-start | bytes 393224 | tf_op jit(solution)/shard_map/ppermute | solution.py:228
  109.8 10.2 %collective-permute-start.30 = (bf16[128,512]{1,0:T(8,128)(2,1)S(1)}, bf16[128,512]{1,0:T(8,128)(2,1)S(1)}, u32[]{:S(2)}, u32[]{:S(2)}) collective-permute-start(bf16[128,512]{1,0:T(8,128)(2,1)S(1)} %get-tuple-element.70.refs_0_), channel_id=1, source_target_pairs={{0,4},{1,5},{2,6},{3,7},{4,0},{5,1},{6,2},{7,3},{8,12},{9,13},{10,... | collective-permute-start | bytes 393224 | tf_op jit(solution)/shard_map/ppermute | solution.py:218
  112.5 7.6 %collective-permute-start.31 = (bf16[128,512]{1,0:T(8,128)(2,1)S(1)}, bf16[128,512]{1,0:T(8,128)(2,1)S(1)}, u32[]{:S(2)}, u32[]{:S(2)}) collective-permute-start(bf16[128,512]{1,0:T(8,128)(2,1)S(1)} %get-tuple-element.69), channel_id=1, source_target_pairs={{0,2},{1,3},{2,0},{3,1},{4,6},{5,7},{6,4},{7,5},{8,10},{9,11},{10,... | collective-permute-start | bytes 393224 | tf_op jit(solution)/shard_map/ppermute | solution.py:218
  112.6 10.9 %collective-permute-start.29 = (bf16[128,512]{1,0:T(8,128)(2,1)S(1)}, bf16[128,512]{1,0:T(8,128)(2,1)S(1)}, u32[]{:S(2)}, u32[]{:S(2)}) collective-permute-start(bf16[128,512]{1,0:T(8,128)(2,1)S(1)} %get-tuple-element.69), channel_id=1, source_target_pairs={{0,6},{1,7},{2,4},{3,5},{4,2},{5,3},{6,0},{7,1},{8,14},{9,15},{10,... | collective-permute-start | bytes 393224 | tf_op jit(solution)/shard_map/ppermute | solution.py:218
  123.8 8.4 %collective-permute-start.34 = (bf16[128,512]{1,0:T(8,128)(2,1)S(1)}, bf16[128,512]{1,0:T(8,128)(2,1)S(1)}, u32[]{:S(2)}, u32[]{:S(2)}) collective-permute-start(bf16[128,512]{1,0:T(8,128)(2,1)S(1)} %get-tuple-element.72), channel_id=1, source_target_pairs={{0,8},{1,9},{2,10},{3,11},{4,12},{5,13},{6,14},{7,15},{8,16},{9,17... | collective-permute-start | bytes 393224 | tf_op jit(solution)/shard_map/ppermute | solution.py:228
  123.9 8.4 %collective-permute-start.32 = (bf16[128,512]{1,0:T(8,128)(2,1)S(1)}, bf16[128,512]{1,0:T(8,128)(2,1)S(1)}, u32[]{:S(2)}, u32[]{:S(2)}) collective-permute-start(bf16[128,512]{1,0:T(8,128)(2,1)S(1)} %get-tuple-element.71), channel_id=1, source_target_pairs={{0,10},{1,11},{2,8},{3,9},{4,14},{5,15},{6,12},{7,13},{8,18},{9,19... | collective-permute-start | bytes 393224 | tf_op jit(solution)/shard_map/ppermute | solution.py:228
  134.6 10.3 %collective-permute-start.37 = (bf16[128,512]{1,0:T(8,128)(2,1)S(1)}, bf16[128,512]{1,0:T(8,128)(2,1)S(1)}, u32[]{:S(2)}, u32[]{:S(2)}) collective-permute-start(bf16[128,512]{1,0:T(8,128)(2,1)S(1)} %get-tuple-element.74.refs_0_), channel_id=1, source_target_pairs={{0,4},{1,5},{2,6},{3,7},{4,0},{5,1},{6,2},{7,3},{8,12},{9,13},{10,... | collective-permute-start | bytes 393224 | tf_op jit(solution)/shard_map/ppermute | solution.py:218
  137.2 7.7 %collective-permute-start.38 = (bf16[128,512]{1,0:T(8,128)(2,1)S(1)}, bf16[128,512]{1,0:T(8,128)(2,1)S(1)}, u32[]{:S(2)}, u32[]{:S(2)}) collective-permute-start(bf16[128,512]{1,0:T(8,128)(2,1)S(1)} %get-tuple-element.73), channel_id=1, source_target_pairs={{0,2},{1,3},{2,0},{3,1},{4,6},{5,7},{6,4},{7,5},{8,10},{9,11},{10,... | collective-permute-start | bytes 393224 | tf_op jit(solution)/shard_map/ppermute | solution.py:218
  137.3 10.9 %collective-permute-start.36 = (bf16[128,512]{1,0:T(8,128)(2,1)S(1)}, bf16[128,512]{1,0:T(8,128)(2,1)S(1)}, u32[]{:S(2)}, u32[]{:S(2)}) collective-permute-start(bf16[128,512]{1,0:T(8,128)(2,1)S(1)} %get-tuple-element.73), channel_id=1, source_target_pairs={{0,6},{1,7},{2,4},{3,5},{4,2},{5,3},{6,0},{7,1},{8,14},{9,15},{10,... | collective-permute-start | bytes 393224 | tf_op jit(solution)/shard_map/ppermute | solution.py:218
  148.5 8.4 %collective-permute-start.41 = (bf16[128,512]{1,0:T(8,128)(2,1)S(1)}, bf16[128,512]{1,0:T(8,128)(2,1)S(1)}, u32[]{:S(2)}, u32[]{:S(2)}) collective-permute-start(bf16[128,512]{1,0:T(8,128)(2,1)S(1)} %get-tuple-element.76), channel_id=1, source_target_pairs={{0,8},{1,9},{2,10},{3,11},{4,12},{5,13},{6,14},{7,15},{8,16},{9,17... | collective-permute-start | bytes 393224 | tf_op jit(solution)/shard_map/ppermute | solution.py:228
  148.6 8.4 %collective-permute-start.39 = (bf16[128,512]{1,0:T(8,128)(2,1)S(1)}, bf16[128,512]{1,0:T(8,128)(2,1)S(1)}, u32[]{:S(2)}, u32[]{:S(2)}) collective-permute-start(bf16[128,512]{1,0:T(8,128)(2,1)S(1)} %get-tuple-element.75), channel_id=1, source_target_pairs={{0,10},{1,11},{2,8},{3,9},{4,14},{5,15},{6,12},{7,13},{8,18},{9,19... | collective-permute-start | bytes 393224 | tf_op jit(solution)/shard_map/ppermute | solution.py:228
  159.2 10.2 %collective-permute-start.44 = (bf16[128,512]{1,0:T(8,128)(2,1)S(1)}, bf16[128,512]{1,0:T(8,128)(2,1)S(1)}, u32[]{:S(2)}, u32[]{:S(2)}) collective-permute-start(bf16[128,512]{1,0:T(8,128)(2,1)S(1)} %get-tuple-element.78.refs_0_), channel_id=1, source_target_pairs={{0,4},{1,5},{2,6},{3,7},{4,0},{5,1},{6,2},{7,3},{8,12},{9,13},{10,... | collective-permute-start | bytes 393224 | tf_op jit(solution)/shard_map/ppermute | solution.py:218
  161.9 7.6 %collective-permute-start.45 = (bf16[128,512]{1,0:T(8,128)(2,1)S(1)}, bf16[128,512]{1,0:T(8,128)(2,1)S(1)}, u32[]{:S(2)}, u32[]{:S(2)}) collective-permute-start(bf16[128,512]{1,0:T(8,128)(2,1)S(1)} %get-tuple-element.77), channel_id=1, source_target_pairs={{0,2},{1,3},{2,0},{3,1},{4,6},{5,7},{6,4},{7,5},{8,10},{9,11},{10,... | collective-permute-start | bytes 393224 | tf_op jit(solution)/shard_map/ppermute | solution.py:218
  162.0 10.9 %collective-permute-start.43 = (bf16[128,512]{1,0:T(8,128)(2,1)S(1)}, bf16[128,512]{1,0:T(8,128)(2,1)S(1)}, u32[]{:S(2)}, u32[]{:S(2)}) collective-permute-start(bf16[128,512]{1,0:T(8,128)(2,1)S(1)} %get-tuple-element.77), channel_id=1, source_target_pairs={{0,6},{1,7},{2,4},{3,5},{4,2},{5,3},{6,0},{7,1},{8,14},{9,15},{10,... | collective-permute-start | bytes 393224 | tf_op jit(solution)/shard_map/ppermute | solution.py:218
  (18 other events, 43.3 us)

commit v3 on v2

--- a/solution.py
+++ b/solution.py
@@ -14,7 +14,7 @@
 TABLE = pl.BlockSpec(memory_space=pltpu.SMEM)
 
 
-def place_kernel(layer, order, column_ref, slot_ref, bias_ref, index_ref, weights_ref, placed_ref, row_ref, held, tile_ref, arrived, listed):
+def place_kernel(layer, order, column_ref, slot_ref, index_ref, weights_ref, placed_ref, held, tile_ref, arrived, listed):
     slots, tile, width = held.shape
     lanes = 2 * tile
     copies = arrived.shape[0]
@@ -41,8 +41,6 @@
     listing.start()
     for part in range(copies):
         copy(part).start()
-    for spot in range(slots):
-        row_ref[:, pl.ds(spot * tile, tile)] = bias_ref[layer, pl.ds(slot_ref[spot], 1), :]
     listing.wait()
     for part in range(copies):
         copy(part).wait()
@@ -50,17 +48,14 @@
             place(pair)
 
 
-def placed(layer, weights, biases, tile_index, columns, slots_of, order, copies):
+def placed(layer, weights, tile_index, columns, slots_of, order, copies):
     _, slots, tile, width = weights.shape
     away = pl.BlockSpec(memory_space=pltpu.HBM)
     return pl.pallas_call(
         functools.partial(place_kernel, layer, order),
-        in_specs=[TABLE, TABLE, WHOLE, away, away],
-        out_specs=[WHOLE, WHOLE],
-        out_shape=[
-            jax.ShapeDtypeStruct((slots // 2, width, 2 * tile), weights.dtype),
-            jax.ShapeDtypeStruct((1, slots * tile), biases.dtype),
-        ],
+        in_specs=[TABLE, TABLE, away, away],
+        out_specs=WHOLE,
+        out_shape=jax.ShapeDtypeStruct((slots // 2, width, 2 * tile), weights.dtype),
         scratch_shapes=[
             pltpu.VMEM((slots, tile, width), weights.dtype),
             pltpu.SMEM(tile_index.shape[1:], tile_index.dtype),
@@ -69,7 +64,32 @@
         ],
         compiler_params=pltpu.CompilerParams(vmem_limit_bytes=PLACE_VMEM),
         name="place_tiles",
-    )(columns, slots_of, biases, tile_index, weights)
+    )(columns, slots_of, tile_index, weights)
+
+
+def rows_kernel(group, bias_ref, place_ref, *row_refs):
+    _, slots, tile = bias_ref.shape
+    deep = slots // group
+    near = place_ref[1, :1, :tile]
+    for layer, row_ref in enumerate(row_refs):
+        for spot in range(slots):
+            x, d = spot // deep, spot % deep
+            value = bias_ref[layer, pl.ds(d * group + x, 1), :]
+            for digit in range(1, group):
+                value = jnp.where(near == digit, bias_ref[layer, pl.ds(d * group + (x ^ digit), 1), :], value)
+            row_ref[:, pl.ds(spot * tile, tile)] = value
+
+
+def rows_of(biases, place, group):
+    layers, slots, tile = biases.shape
+    return pl.pallas_call(
+        functools.partial(rows_kernel, group),
+        in_specs=[WHOLE] * 2,
+        out_specs=[WHOLE] * layers,
+        out_shape=[jax.ShapeDtypeStruct((1, slots * tile), biases.dtype)] * layers,
+        compiler_params=pltpu.CompilerParams(vmem_limit_bytes=LAYER_VMEM),
+        name="bias_rows",
+    )(biases, place)
 
 
 def turn_kernel(micro, *refs):
@@ -212,7 +232,8 @@
     order = sorted(range(local // 2), key=lambda pair: (2 * pair % deep, pair))
     place = jnp.broadcast_to(jnp.stack([segment, near]).astype(jnp.int32)[:, None, None], (2, 8, max(batch, 4 * tile)))
     columns, slots_of, place, first = lax.optimization_barrier((columns, slots_of, place, segment == 0))
-    layers = [placed(index, weights, biases, tile_index, columns, slots_of, order, copies) for index in range(2)]
+    matrices = [placed(index, weights, tile_index, columns, slots_of, order, copies) for index in range(2)]
+    layers = list(zip(matrices, rows_of(biases, place, group)))
 
     def along(value, flip):
         return lax.ppermute(value, "blk", [(i, i ^ flip) for i in range(devices)])

time: 179 us -> 182 us (1.017)
  waiting for transfers between devices: 89.5 us -> 91.7 us
    ppermute x12, waiting for transfers between devices: 24.6 us -> 27 us  [passed(): lax.ppermute(part, ('segment', 'blk'), [(s * devices + i, (s + 1) % segme...]
  transfers between devices with their start and end apart: 47 -> 47, of which waited for: 28 -> 32; matrix products, arithmetic and copies ran while one was open for 0% -> 0% of each run, Pallas kernels for 9% -> 9%
where the time goes in v3:
time: 182 us; the launch traced here: 181 us
  waiting for transfers between devices  91.7 us (50%)
  starting transfers between devices  65.5 us (36%)
  Pallas kernels  22 us (12%)
    ppermute x35, waiting for transfers between devices, along(): return lax.ppermute(value, 'blk', [(i, i ^ flip) for i in range(devices)])  64.7 us
    ppermute x35, starting transfers between devices, along(): return lax.ppermute(value, 'blk', [(i, i ^ flip) for i in range(devices)])  38.3 us
    ppermute x12, starting transfers between devices, passed(): lax.ppermute(part, ('segment', 'blk'), [(s * devices + i, (s + 1) % segme...  27.2 us
    ppermute x12, waiting for transfers between devices, passed(): lax.ppermute(part, ('segment', 'blk'), [(s * devices + i, (s + 1) % segme...  27 us
    pallas_call x13, Pallas kernels, layer(): pl.pallas_call(early_kernel, in_specs=[WHOLE] * (len(early) + 2), out_spe...  8.03 us
    pallas_call x2, Pallas kernels, placed(): pl.pallas_call(functools.partial(place_kernel, layer, order), in_specs=[T...  7.68 us
    pallas_call x14, Pallas kernels, layer(): pl.pallas_call(functools.partial(layer_kernel, len(pieces), outs, depth,...  4.81 us
  transfers between devices with their start and end apart: 47, of which 32 were waited for; matrix products, arithmetic and copies ran while one was open for 0% of the time, Pallas kernels for 9%

profile of v3, /device:TPU:0, one launch (start us, length us, event | category | flops | bytes accessed | tf_op | source)
XLA Modules:
  0.0 181.3 jit_solution(14055868383399740100)
XLA Ops:
  2.2 3.6 %place_tiles.2.refs_2_.refs_3_.refs_1_ = bf16[8,2048,128]{2,1,0:T(8,128)(2,1)S(1)} custom-call(s32[2,32]{1,0:T(2,128)S(1)} %pad_add_fusion.column_ref, s32[16]{0:T(128)S(1)} %fusion.3.slot_ref, s32[2,16,32]{2,1,0:T(8,128)S(1)} %copy-done.1, bf16[2,16,64,2048]{3,2,1,0:T(8,128)(2,1)} %weights_ref.3), custom_call_target="tpu_custom_call" | custom-call | tf_op jit(solution)/shard_map/place_tiles/pallas_call | solution.py:54
  6.8 3.7 %collective-permute-start.2 = (bf16[128,512]{1,0:T(8,128)(2,1)S(1)}, bf16[128,512]{1,0:T(8,128)(2,1)S(1)}, u32[]{:S(2)}, u32[]{:S(2)}) collective-permute-start(bf16[128,512]{1,0:T(8,128)(2,1)S(1)} %get-tuple-element.49.refs_0_), channel_id=1, source_target_pairs={{0,4},{1,5},{2,6},{3,7},{4,0},{5,1},{6,2},{7,3},{8,12},{9,13},{10,... | collective-permute-start | bytes 393224 | tf_op jit(solution)/shard_map/ppermute | solution.py:239
  12.0 4.0 %place_tiles.3.refs_3_.refs_1_ = bf16[8,2048,128]{2,1,0:T(8,128)(2,1)S(1)} custom-call(s32[2,32]{1,0:T(2,128)S(1)} %pad_add_fusion.column_ref, s32[16]{0:T(128)S(1)} %fusion.3.slot_ref, s32[2,16,32]{2,1,0:T(8,128)S(1)} %copy-done.1, bf16[2,16,64,2048]{3,2,1,0:T(8,128)(2,1)} %weights_ref.3), custom_call_target="tpu_custom_call" | custom-call | tf_op jit(solution)/shard_map/place_tiles/pallas_call | solution.py:54
  18.3 3.1 %collective-permute-done.1.refs_0_ = bf16[128,512]{1,0:T(8,128)(2,1)S(1)} collective-permute-done((bf16[128,512]{1,0:T(8,128)(2,1)S(1)}, bf16[128,512]{1,0:T(8,128)(2,1)S(1)}, u32[]{:S(2)}, u32[]{:S(2)}) %collective-permute-start.1) | collective-permute-done | bytes 131104 | tf_op jit(solution)/shard_map/ppermute | solution.py:239
  21.7 3.3 %collective-permute-start.4 = (bf16[128,512]{1,0:T(8,128)(2,1)S(1)}, bf16[128,512]{1,0:T(8,128)(2,1)S(1)}, u32[]{:S(2)}, u32[]{:S(2)}) collective-permute-start(bf16[128,512]{1,0:T(8,128)(2,1)S(1)} %get-tuple-element.51), channel_id=1, source_target_pairs={{0,10},{1,11},{2,8},{3,9},{4,14},{5,15},{6,12},{7,13},{8,18},{9,19... | collective-permute-start | bytes 393224 | tf_op jit(solution)/shard_map/ppermute | solution.py:249
  26.7 3.2 %collective-permute-done.4 = bf16[128,512]{1,0:T(8,128)(2,1)S(1)} collective-permute-done((bf16[128,512]{1,0:T(8,128)(2,1)S(1)}, bf16[128,512]{1,0:T(8,128)(2,1)S(1)}, u32[]{:S(2)}, u32[]{:S(2)}) %collective-permute-start.4) | collective-permute-done | bytes 131104 | tf_op jit(solution)/shard_map/ppermute | solution.py:249
  29.8 2.7 %collective-permute-done.6 = bf16[128,512]{1,0:T(8,128)(2,1)S(1)} collective-permute-done((bf16[128,512]{1,0:T(8,128)(2,1)S(1)}, bf16[128,512]{1,0:T(8,128)(2,1)S(1)}, u32[]{:S(2)}, u32[]{:S(2)}) %collective-permute-start.6) | collective-permute-done | bytes 131104 | tf_op jit(solution)/shard_map/ppermute | solution.py:249
  35.8 3.1 %collective-permute-start.9 = (bf16[128,512]{1,0:T(8,128)(2,1)S(1)}, bf16[128,512]{1,0:T(8,128)(2,1)S(1)}, u32[]{:S(2)}, u32[]{:S(2)}) collective-permute-start(bf16[128,512]{1,0:T(8,128)(2,1)S(1)} %get-tuple-element.54.refs_0_), channel_id=1, source_target_pairs={{0,4},{1,5},{2,6},{3,7},{4,0},{5,1},{6,2},{7,3},{8,12},{9,13},{10,... | collective-permute-start | bytes 393224 | tf_op jit(solution)/shard_map/ppermute | solution.py:239
  39.4 3.5 %collective-permute-done.10.refs_2_ = bf16[128,512]{1,0:T(8,128)(2,1)S(1)} collective-permute-done((bf16[128,512]{1,0:T(8,128)(2,1)S(1)}, bf16[128,512]{1,0:T(8,128)(2,1)S(1)}, u32[]{:S(2)}, u32[]{:S(2)}) %collective-permute-start.10) | collective-permute-done | bytes 131104 | tf_op jit(solution)/shard_map/ppermute | solution.py:239
  42.9 6.0 %collective-permute-done.9.refs_1_ = bf16[128,512]{1,0:T(8,128)(2,1)S(1)} collective-permute-done((bf16[128,512]{1,0:T(8,128)(2,1)S(1)}, bf16[128,512]{1,0:T(8,128)(2,1)S(1)}, u32[]{:S(2)}, u32[]{:S(2)}) %collective-permute-start.9) | collective-permute-done | bytes 131104 | tf_op jit(solution)/shard_map/ppermute | solution.py:239
  54.0 2.9 %collective-permute-done.11 = bf16[128,512]{1,0:T(8,128)(2,1)S(1)} collective-permute-done((bf16[128,512]{1,0:T(8,128)(2,1)S(1)}, bf16[128,512]{1,0:T(8,128)(2,1)S(1)}, u32[]{:S(2)}, u32[]{:S(2)}) %collective-permute-start.11) | collective-permute-done | bytes 131104 | tf_op jit(solution)/shard_map/ppermute | solution.py:249
  60.8 3.5 %collective-permute-start.16 = (bf16[128,512]{1,0:T(8,128)(2,1)S(1)}, bf16[128,512]{1,0:T(8,128)(2,1)S(1)}, u32[]{:S(2)}, u32[]{:S(2)}) collective-permute-start(bf16[128,512]{1,0:T(8,128)(2,1)S(1)} %get-tuple-element.58.refs_0_), channel_id=1, source_target_pairs={{0,4},{1,5},{2,6},{3,7},{4,0},{5,1},{6,2},{7,3},{8,12},{9,13},{10,... | collective-permute-start | bytes 393224 | tf_op jit(solution)/shard_map/ppermute | solution.py:239
  65.8 6.1 %collective-permute-done.16.refs_1_ = bf16[128,512]{1,0:T(8,128)(2,1)S(1)} collective-permute-done((bf16[128,512]{1,0:T(8,128)(2,1)S(1)}, bf16[128,512]{1,0:T(8,128)(2,1)S(1)}, u32[]{:S(2)}, u32[]{:S(2)}) %collective-permute-start.16) | collective-permute-done | bytes 131104 | tf_op jit(solution)/shard_map/ppermute | solution.py:239
  74.8 2.7 %collective-permute-start.18 = (bf16[128,512]{1,0:T(8,128)(2,1)S(1)}, bf16[128,512]{1,0:T(8,128)(2,1)S(1)}, u32[]{:S(2)}, u32[]{:S(2)}) collective-permute-start(bf16[128,512]{1,0:T(8,128)(2,1)S(1)} %get-tuple-element.59), channel_id=1, source_target_pairs={{0,10},{1,11},{2,8},{3,9},{4,14},{5,15},{6,12},{7,13},{8,18},{9,19... | collective-permute-start | bytes 393224 | tf_op jit(solution)/shard_map/ppermute | solution.py:249
  81.8 2.7 %collective-permute-done.20 = bf16[128,512]{1,0:T(8,128)(2,1)S(1)} collective-permute-done((bf16[128,512]{1,0:T(8,128)(2,1)S(1)}, bf16[128,512]{1,0:T(8,128)(2,1)S(1)}, u32[]{:S(2)}, u32[]{:S(2)}) %collective-permute-start.20) | collective-permute-done | bytes 131104 | tf_op jit(solution)/shard_map/ppermute | solution.py:249
  86.9 2.8 %collective-permute-start.23 = (bf16[128,512]{1,0:T(8,128)(2,1)S(1)}, bf16[128,512]{1,0:T(8,128)(2,1)S(1)}, u32[]{:S(2)}, u32[]{:S(2)}) collective-permute-start(bf16[128,512]{1,0:T(8,128)(2,1)S(1)} %get-tuple-element.62.refs_0_), channel_id=1, source_target_pairs={{0,4},{1,5},{2,6},{3,7},{4,0},{5,1},{6,2},{7,3},{8,12},{9,13},{10,... | collective-permute-start | bytes 393224 | tf_op jit(solution)/shard_map/ppermute | solution.py:239
  91.3 5.7 %collective-permute-done.23.refs_1_ = bf16[128,512]{1,0:T(8,128)(2,1)S(1)} collective-permute-done((bf16[128,512]{1,0:T(8,128)(2,1)S(1)}, bf16[128,512]{1,0:T(8,128)(2,1)S(1)}, u32[]{:S(2)}, u32[]{:S(2)}) %collective-permute-start.23) | collective-permute-done | bytes 131104 | tf_op jit(solution)/shard_map/ppermute | solution.py:239
  97.7 2.9 %collective-permute-done.22.refs_0_ = bf16[128,512]{1,0:T(8,128)(2,1)S(1)} collective-permute-done((bf16[128,512]{1,0:T(8,128)(2,1)S(1)}, bf16[128,512]{1,0:T(8,128)(2,1)S(1)}, u32[]{:S(2)}, u32[]{:S(2)}) %collective-permute-start.22) | collective-permute-done | bytes 131104 | tf_op jit(solution)/shard_map/ppermute | solution.py:239
  101.0 4.3 %collective-permute-start.25 = (bf16[128,512]{1,0:T(8,128)(2,1)S(1)}, bf16[128,512]{1,0:T(8,128)(2,1)S(1)}, u32[]{:S(2)}, u32[]{:S(2)}) collective-permute-start(bf16[128,512]{1,0:T(8,128)(2,1)S(1)} %get-tuple-element.63), channel_id=1, source_target_pairs={{0,10},{1,11},{2,8},{3,9},{4,14},{5,15},{6,12},{7,13},{8,18},{9,19... | collective-permute-start | bytes 393224 | tf_op jit(solution)/shard_map/ppermute | solution.py:249
  105.3 4.2 %collective-permute-done.27.refs_0_.refs_4_ = bf16[128,512]{1,0:T(8,128)(2,1)S(1)} collective-permute-done((bf16[128,512]{1,0:T(8,128)(2,1)S(1)}, bf16[128,512]{1,0:T(8,128)(2,1)S(1)}, u32[]{:S(2)}, u32[]{:S(2)}) %collective-permute-start.27) | collective-permute-done | bytes 131104 | tf_op jit(solution)/shard_map/ppermute | solution.py:249
  111.7 2.9 %collective-permute-start.30 = (bf16[128,512]{1,0:T(8,128)(2,1)S(1)}, bf16[128,512]{1,0:T(8,128)(2,1)S(1)}, u32[]{:S(2)}, u32[]{:S(2)}) collective-permute-start(bf16[128,512]{1,0:T(8,128)(2,1)S(1)} %get-tuple-element.66.refs_0_), channel_id=1, source_target_pairs={{0,4},{1,5},{2,6},{3,7},{4,0},{5,1},{6,2},{7,3},{8,12},{9,13},{10,... | collective-permute-start | bytes 393224 | tf_op jit(solution)/shard_map/ppermute | solution.py:239
  116.2 5.7 %collective-permute-done.30.refs_1_ = bf16[128,512]{1,0:T(8,128)(2,1)S(1)} collective-permute-done((bf16[128,512]{1,0:T(8,128)(2,1)S(1)}, bf16[128,512]{1,0:T(8,128)(2,1)S(1)}, u32[]{:S(2)}, u32[]{:S(2)}) %collective-permute-start.30) | collective-permute-done | bytes 131104 | tf_op jit(solution)/shard_map/ppermute | solution.py:239
  122.6 2.9 %collective-permute-done.29.refs_0_ = bf16[128,512]{1,0:T(8,128)(2,1)S(1)} collective-permute-done((bf16[128,512]{1,0:T(8,128)(2,1)S(1)}, bf16[128,512]{1,0:T(8,128)(2,1)S(1)}, u32[]{:S(2)}, u32[]{:S(2)}) %collective-permute-start.29) | collective-permute-done | bytes 131104 | tf_op jit(solution)/shard_map/ppermute | solution.py:239
  125.8 4.6 %collective-permute-start.32 = (bf16[128,512]{1,0:T(8,128)(2,1)S(1)}, bf16[128,512]{1,0:T(8,128)(2,1)S(1)}, u32[]{:S(2)}, u32[]{:S(2)}) collective-permute-start(bf16[128,512]{1,0:T(8,128)(2,1)S(1)} %get-tuple-element.67), channel_id=1, source_target_pairs={{0,10},{1,11},{2,8},{3,9},{4,14},{5,15},{6,12},{7,13},{8,18},{9,19... | collective-permute-start | bytes 393224 | tf_op jit(solution)/shard_map/ppermute | solution.py:249
  130.4 4.1 %collective-permute-done.34.refs_0_.refs_4_ = bf16[128,512]{1,0:T(8,128)(2,1)S(1)} collective-permute-done((bf16[128,512]{1,0:T(8,128)(2,1)S(1)}, bf16[128,512]{1,0:T(8,128)(2,1)S(1)}, u32[]{:S(2)}, u32[]{:S(2)}) %collective-permute-start.34) | collective-permute-done | bytes 131104 | tf_op jit(solution)/shard_map/ppermute | solution.py:249
  136.8 2.5 %collective-permute-start.37 = (bf16[128,512]{1,0:T(8,128)(2,1)S(1)}, bf16[128,512]{1,0:T(8,128)(2,1)S(1)}, u32[]{:S(2)}, u32[]{:S(2)}) collective-permute-start(bf16[128,512]{1,0:T(8,128)(2,1)S(1)} %get-tuple-element.70.refs_0_), channel_id=1, source_target_pairs={{0,4},{1,5},{2,6},{3,7},{4,0},{5,1},{6,2},{7,3},{8,12},{9,13},{10,... | collective-permute-start | bytes 393224 | tf_op jit(solution)/shard_map/ppermute | solution.py:239
  141.2 5.7 %collective-permute-done.37.refs_1_ = bf16[128,512]{1,0:T(8,128)(2,1)S(1)} collective-permute-done((bf16[128,512]{1,0:T(8,128)(2,1)S(1)}, bf16[128,512]{1,0:T(8,128)(2,1)S(1)}, u32[]{:S(2)}, u32[]{:S(2)}) %collective-permute-start.37) | collective-permute-done | bytes 131104 | tf_op jit(solution)/shard_map/ppermute | solution.py:239
  147.6 2.9 %collective-permute-done.36.refs_0_ = bf16[128,512]{1,0:T(8,128)(2,1)S(1)} collective-permute-done((bf16[128,512]{1,0:T(8,128)(2,1)S(1)}, bf16[128,512]{1,0:T(8,128)(2,1)S(1)}, u32[]{:S(2)}, u32[]{:S(2)}) %collective-permute-start.36) | collective-permute-done | bytes 131104 | tf_op jit(solution)/shard_map/ppermute | solution.py:239
  150.9 4.2 %collective-permute-start.39 = (bf16[128,512]{1,0:T(8,128)(2,1)S(1)}, bf16[128,512]{1,0:T(8,128)(2,1)S(1)}, u32[]{:S(2)}, u32[]{:S(2)}) collective-permute-start(bf16[128,512]{1,0:T(8,128)(2,1)S(1)} %get-tuple-element.71), channel_id=1, source_target_pairs={{0,10},{1,11},{2,8},{3,9},{4,14},{5,15},{6,12},{7,13},{8,18},{9,19... | collective-permute-start | bytes 393224 | tf_op jit(solution)/shard_map/ppermute | solution.py:249
  155.2 4.1 %collective-permute-done.41.refs_0_.refs_4_ = bf16[128,512]{1,0:T(8,128)(2,1)S(1)} collective-permute-done((bf16[128,512]{1,0:T(8,128)(2,1)S(1)}, bf16[128,512]{1,0:T(8,128)(2,1)S(1)}, u32[]{:S(2)}, u32[]{:S(2)}) %collective-permute-start.41) | collective-permute-done | bytes 131104 | tf_op jit(solution)/shard_map/ppermute | solution.py:249
  166.0 5.9 %collective-permute-done.44.refs_1_ = bf16[128,512]{1,0:T(8,128)(2,1)S(1)} collective-permute-done((bf16[128,512]{1,0:T(8,128)(2,1)S(1)}, bf16[128,512]{1,0:T(8,128)(2,1)S(1)}, u32[]{:S(2)}, u32[]{:S(2)}) %collective-permute-start.44) | collective-permute-done | bytes 131104 | tf_op jit(solution)/shard_map/ppermute | solution.py:239
  177.5 3.0 %collective-permute-done.46.refs_2_ = bf16[128,512]{1,0:T(8,128)(2,1)S(1)} collective-permute-done((bf16[128,512]{1,0:T(8,128)(2,1)S(1)}, bf16[128,512]{1,0:T(8,128)(2,1)S(1)}, u32[]{:S(2)}, u32[]{:S(2)}) %collective-permute-start.46) | collective-permute-done | bytes 131104 | tf_op jit(solution)/shard_map/ppermute | solution.py:239
  (111 shorter events, 58.2 us)
Async XLA Ops:
  6.8 10.9 %collective-permute-start.2 = (bf16[128,512]{1,0:T(8,128)(2,1)S(1)}, bf16[128,512]{1,0:T(8,128)(2,1)S(1)}, u32[]{:S(2)}, u32[]{:S(2)}) collective-permute-start(bf16[128,512]{1,0:T(8,128)(2,1)S(1)} %get-tuple-element.49.refs_0_), channel_id=1, source_target_pairs={{0,4},{1,5},{2,6},{3,7},{4,0},{5,1},{6,2},{7,3},{8,12},{9,13},{10,... | collective-permute-start | bytes 393224 | tf_op jit(solution)/shard_map/ppermute | solution.py:239
  10.4 7.3 %collective-permute-start.3 = (bf16[128,512]{1,0:T(8,128)(2,1)S(1)}, bf16[128,512]{1,0:T(8,128)(2,1)S(1)}, u32[]{:S(2)}, u32[]{:S(2)}) collective-permute-start(bf16[128,512]{1,0:T(8,128)(2,1)S(1)} %get-tuple-element.48), channel_id=1, source_target_pairs={{0,2},{1,3},{2,0},{3,1},{4,6},{5,7},{6,4},{7,5},{8,10},{9,11},{10,... | collective-permute-start | bytes 393224 | tf_op jit(solution)/shard_map/ppermute | solution.py:239
  12.0 9.4 %collective-permute-start.1 = (bf16[128,512]{1,0:T(8,128)(2,1)S(1)}, bf16[128,512]{1,0:T(8,128)(2,1)S(1)}, u32[]{:S(2)}, u32[]{:S(2)}) collective-permute-start(bf16[128,512]{1,0:T(8,128)(2,1)S(1)} %get-tuple-element.48), channel_id=1, source_target_pairs={{0,6},{1,7},{2,4},{3,5},{4,2},{5,3},{6,0},{7,1},{8,14},{9,15},{10,... | collective-permute-start | bytes 393224 | tf_op jit(solution)/shard_map/ppermute | solution.py:239
  21.7 8.1 %collective-permute-start.4 = (bf16[128,512]{1,0:T(8,128)(2,1)S(1)}, bf16[128,512]{1,0:T(8,128)(2,1)S(1)}, u32[]{:S(2)}, u32[]{:S(2)}) collective-permute-start(bf16[128,512]{1,0:T(8,128)(2,1)S(1)} %get-tuple-element.51), channel_id=1, source_target_pairs={{0,10},{1,11},{2,8},{3,9},{4,14},{5,15},{6,12},{7,13},{8,18},{9,19... | collective-permute-start | bytes 393224 | tf_op jit(solution)/shard_map/ppermute | solution.py:249
  25.1 7.5 %collective-permute-start.6 = (bf16[128,512]{1,0:T(8,128)(2,1)S(1)}, bf16[128,512]{1,0:T(8,128)(2,1)S(1)}, u32[]{:S(2)}, u32[]{:S(2)}) collective-permute-start(bf16[128,512]{1,0:T(8,128)(2,1)S(1)} %get-tuple-element.52), channel_id=1, source_target_pairs={{0,8},{1,9},{2,10},{3,11},{4,12},{5,13},{6,14},{7,15},{8,16},{9,17... | collective-permute-start | bytes 393224 | tf_op jit(solution)/shard_map/ppermute | solution.py:249
  34.9 8.0 %collective-permute-start.10 = (bf16[128,512]{1,0:T(8,128)(2,1)S(1)}, bf16[128,512]{1,0:T(8,128)(2,1)S(1)}, u32[]{:S(2)}, u32[]{:S(2)}) collective-permute-start(bf16[128,512]{1,0:T(8,128)(2,1)S(1)} %get-tuple-element.53), channel_id=1, source_target_pairs={{0,2},{1,3},{2,0},{3,1},{4,6},{5,7},{6,4},{7,5},{8,10},{9,11},{10,... | collective-permute-start | bytes 393224 | tf_op jit(solution)/shard_map/ppermute | solution.py:239
  35.8 13.1 %collective-permute-start.9 = (bf16[128,512]{1,0:T(8,128)(2,1)S(1)}, bf16[128,512]{1,0:T(8,128)(2,1)S(1)}, u32[]{:S(2)}, u32[]{:S(2)}) collective-permute-start(bf16[128,512]{1,0:T(8,128)(2,1)S(1)} %get-tuple-element.54.refs_0_), channel_id=1, source_target_pairs={{0,4},{1,5},{2,6},{3,7},{4,0},{5,1},{6,2},{7,3},{8,12},{9,13},{10,... | collective-permute-start | bytes 393224 | tf_op jit(solution)/shard_map/ppermute | solution.py:239
  39.0 10.6 %collective-permute-start.8 = (bf16[128,512]{1,0:T(8,128)(2,1)S(1)}, bf16[128,512]{1,0:T(8,128)(2,1)S(1)}, u32[]{:S(2)}, u32[]{:S(2)}) collective-permute-start(bf16[128,512]{1,0:T(8,128)(2,1)S(1)} %get-tuple-element.53), channel_id=1, source_target_pairs={{0,6},{1,7},{2,4},{3,5},{4,2},{5,3},{6,0},{7,1},{8,14},{9,15},{10,... | collective-permute-start | bytes 393224 | tf_op jit(solution)/shard_map/ppermute | solution.py:239
  49.9 6.9 %collective-permute-start.11 = (bf16[128,512]{1,0:T(8,128)(2,1)S(1)}, bf16[128,512]{1,0:T(8,128)(2,1)S(1)}, u32[]{:S(2)}, u32[]{:S(2)}) collective-permute-start(bf16[128,512]{1,0:T(8,128)(2,1)S(1)} %get-tuple-element.55), channel_id=1, source_target_pairs={{0,10},{1,11},{2,8},{3,9},{4,14},{5,15},{6,12},{7,13},{8,18},{9,19... | collective-permute-start | bytes 393224 | tf_op jit(solution)/shard_map/ppermute | solution.py:249
  60.8 11.2 %collective-permute-start.16 = (bf16[128,512]{1,0:T(8,128)(2,1)S(1)}, bf16[128,512]{1,0:T(8,128)(2,1)S(1)}, u32[]{:S(2)}, u32[]{:S(2)}) collective-permute-start(bf16[128,512]{1,0:T(8,128)(2,1)S(1)} %get-tuple-element.58.refs_0_), channel_id=1, source_target_pairs={{0,4},{1,5},{2,6},{3,7},{4,0},{5,1},{6,2},{7,3},{8,12},{9,13},{10,... | collective-permute-start | bytes 393224 | tf_op jit(solution)/shard_map/ppermute | solution.py:239
  64.3 8.1 %collective-permute-start.17 = (bf16[128,512]{1,0:T(8,128)(2,1)S(1)}, bf16[128,512]{1,0:T(8,128)(2,1)S(1)}, u32[]{:S(2)}, u32[]{:S(2)}) collective-permute-start(bf16[128,512]{1,0:T(8,128)(2,1)S(1)} %get-tuple-element.57), channel_id=1, source_target_pairs={{0,2},{1,3},{2,0},{3,1},{4,6},{5,7},{6,4},{7,5},{8,10},{9,11},{10,... | collective-permute-start | bytes 393224 | tf_op jit(solution)/shard_map/ppermute | solution.py:239
  64.7 9.8 %collective-permute-start.15 = (bf16[128,512]{1,0:T(8,128)(2,1)S(1)}, bf16[128,512]{1,0:T(8,128)(2,1)S(1)}, u32[]{:S(2)}, u32[]{:S(2)}) collective-permute-start(bf16[128,512]{1,0:T(8,128)(2,1)S(1)} %get-tuple-element.57), channel_id=1, source_target_pairs={{0,6},{1,7},{2,4},{3,5},{4,2},{5,3},{6,0},{7,1},{8,14},{9,15},{10,... | collective-permute-start | bytes 393224 | tf_op jit(solution)/shard_map/ppermute | solution.py:239
  74.8 6.9 %collective-permute-start.18 = (bf16[128,512]{1,0:T(8,128)(2,1)S(1)}, bf16[128,512]{1,0:T(8,128)(2,1)S(1)}, u32[]{:S(2)}, u32[]{:S(2)}) collective-permute-start(bf16[128,512]{1,0:T(8,128)(2,1)S(1)} %get-tuple-element.59), channel_id=1, source_target_pairs={{0,10},{1,11},{2,8},{3,9},{4,14},{5,15},{6,12},{7,13},{8,18},{9,19... | collective-permute-start | bytes 393224 | tf_op jit(solution)/shard_map/ppermute | solution.py:249
  77.5 6.9 %collective-permute-start.20 = (bf16[128,512]{1,0:T(8,128)(2,1)S(1)}, bf16[128,512]{1,0:T(8,128)(2,1)S(1)}, u32[]{:S(2)}, u32[]{:S(2)}) collective-permute-start(bf16[128,512]{1,0:T(8,128)(2,1)S(1)} %get-tuple-element.60), channel_id=1, source_target_pairs={{0,8},{1,9},{2,10},{3,11},{4,12},{5,13},{6,14},{7,15},{8,16},{9,17... | collective-permute-start | bytes 393224 | tf_op jit(solution)/shard_map/ppermute | solution.py:249
  86.9 10.2 %collective-permute-start.23 = (bf16[128,512]{1,0:T(8,128)(2,1)S(1)}, bf16[128,512]{1,0:T(8,128)(2,1)S(1)}, u32[]{:S(2)}, u32[]{:S(2)}) collective-permute-start(bf16[128,512]{1,0:T(8,128)(2,1)S(1)} %get-tuple-element.62.refs_0_), channel_id=1, source_target_pairs={{0,4},{1,5},{2,6},{3,7},{4,0},{5,1},{6,2},{7,3},{8,12},{9,13},{10,... | collective-permute-start | bytes 393224 | tf_op jit(solution)/shard_map/ppermute | solution.py:239
  89.7 7.4 %collective-permute-start.24 = (bf16[128,512]{1,0:T(8,128)(2,1)S(1)}, bf16[128,512]{1,0:T(8,128)(2,1)S(1)}, u32[]{:S(2)}, u32[]{:S(2)}) collective-permute-start(bf16[128,512]{1,0:T(8,128)(2,1)S(1)} %get-tuple-element.61), channel_id=1, source_target_pairs={{0,2},{1,3},{2,0},{3,1},{4,6},{5,7},{6,4},{7,5},{8,10},{9,11},{10,... | collective-permute-start | bytes 393224 | tf_op jit(solution)/shard_map/ppermute | solution.py:239
  90.1 10.5 %collective-permute-start.22 = (bf16[128,512]{1,0:T(8,128)(2,1)S(1)}, bf16[128,512]{1,0:T(8,128)(2,1)S(1)}, u32[]{:S(2)}, u32[]{:S(2)}) collective-permute-start(bf16[128,512]{1,0:T(8,128)(2,1)S(1)} %get-tuple-element.61), channel_id=1, source_target_pairs={{0,6},{1,7},{2,4},{3,5},{4,2},{5,3},{6,0},{7,1},{8,14},{9,15},{10,... | collective-permute-start | bytes 393224 | tf_op jit(solution)/shard_map/ppermute | solution.py:239
  100.9 8.5 %collective-permute-start.27 = (bf16[128,512]{1,0:T(8,128)(2,1)S(1)}, bf16[128,512]{1,0:T(8,128)(2,1)S(1)}, u32[]{:S(2)}, u32[]{:S(2)}) collective-permute-start(bf16[128,512]{1,0:T(8,128)(2,1)S(1)} %get-tuple-element.64), channel_id=1, source_target_pairs={{0,8},{1,9},{2,10},{3,11},{4,12},{5,13},{6,14},{7,15},{8,16},{9,17... | collective-permute-start | bytes 393224 | tf_op jit(solution)/shard_map/ppermute | solution.py:249
  101.0 8.5 %collective-permute-start.25 = (bf16[128,512]{1,0:T(8,128)(2,1)S(1)}, bf16[128,512]{1,0:T(8,128)(2,1)S(1)}, u32[]{:S(2)}, u32[]{:S(2)}) collective-permute-start(bf16[128,512]{1,0:T(8,128)(2,1)S(1)} %get-tuple-element.63), channel_id=1, source_target_pairs={{0,10},{1,11},{2,8},{3,9},{4,14},{5,15},{6,12},{7,13},{8,18},{9,19... | collective-permute-start | bytes 393224 | tf_op jit(solution)/shard_map/ppermute | solution.py:249
  111.7 10.2 %collective-permute-start.30 = (bf16[128,512]{1,0:T(8,128)(2,1)S(1)}, bf16[128,512]{1,0:T(8,128)(2,1)S(1)}, u32[]{:S(2)}, u32[]{:S(2)}) collective-permute-start(bf16[128,512]{1,0:T(8,128)(2,1)S(1)} %get-tuple-element.66.refs_0_), channel_id=1, source_target_pairs={{0,4},{1,5},{2,6},{3,7},{4,0},{5,1},{6,2},{7,3},{8,12},{9,13},{10,... | collective-permute-start | bytes 393224 | tf_op jit(solution)/shard_map/ppermute | solution.py:239
  114.7 7.3 %collective-permute-start.31 = (bf16[128,512]{1,0:T(8,128)(2,1)S(1)}, bf16[128,512]{1,0:T(8,128)(2,1)S(1)}, u32[]{:S(2)}, u32[]{:S(2)}) collective-permute-start(bf16[128,512]{1,0:T(8,128)(2,1)S(1)} %get-tuple-element.65), channel_id=1, source_target_pairs={{0,2},{1,3},{2,0},{3,1},{4,6},{5,7},{6,4},{7,5},{8,10},{9,11},{10,... | collective-permute-start | bytes 393224 | tf_op jit(solution)/shard_map/ppermute | solution.py:239
  114.7 10.7 %collective-permute-start.29 = (bf16[128,512]{1,0:T(8,128)(2,1)S(1)}, bf16[128,512]{1,0:T(8,128)(2,1)S(1)}, u32[]{:S(2)}, u32[]{:S(2)}) collective-permute-start(bf16[128,512]{1,0:T(8,128)(2,1)S(1)} %get-tuple-element.65), channel_id=1, source_target_pairs={{0,6},{1,7},{2,4},{3,5},{4,2},{5,3},{6,0},{7,1},{8,14},{9,15},{10,... | collective-permute-start | bytes 393224 | tf_op jit(solution)/shard_map/ppermute | solution.py:239
  125.8 8.7 %collective-permute-start.34 = (bf16[128,512]{1,0:T(8,128)(2,1)S(1)}, bf16[128,512]{1,0:T(8,128)(2,1)S(1)}, u32[]{:S(2)}, u32[]{:S(2)}) collective-permute-start(bf16[128,512]{1,0:T(8,128)(2,1)S(1)} %get-tuple-element.68), channel_id=1, source_target_pairs={{0,8},{1,9},{2,10},{3,11},{4,12},{5,13},{6,14},{7,15},{8,16},{9,17... | collective-permute-start | bytes 393224 | tf_op jit(solution)/shard_map/ppermute | solution.py:249
  125.8 8.7 %collective-permute-start.32 = (bf16[128,512]{1,0:T(8,128)(2,1)S(1)}, bf16[128,512]{1,0:T(8,128)(2,1)S(1)}, u32[]{:S(2)}, u32[]{:S(2)}) collective-permute-start(bf16[128,512]{1,0:T(8,128)(2,1)S(1)} %get-tuple-element.67), channel_id=1, source_target_pairs={{0,10},{1,11},{2,8},{3,9},{4,14},{5,15},{6,12},{7,13},{8,18},{9,19... | collective-permute-start | bytes 393224 | tf_op jit(solution)/shard_map/ppermute | solution.py:249
  136.8 10.2 %collective-permute-start.37 = (bf16[128,512]{1,0:T(8,128)(2,1)S(1)}, bf16[128,512]{1,0:T(8,128)(2,1)S(1)}, u32[]{:S(2)}, u32[]{:S(2)}) collective-permute-start(bf16[128,512]{1,0:T(8,128)(2,1)S(1)} %get-tuple-element.70.refs_0_), channel_id=1, source_target_pairs={{0,4},{1,5},{2,6},{3,7},{4,0},{5,1},{6,2},{7,3},{8,12},{9,13},{10,... | collective-permute-start | bytes 393224 | tf_op jit(solution)/shard_map/ppermute | solution.py:239
  139.3 7.7 %collective-permute-start.38 = (bf16[128,512]{1,0:T(8,128)(2,1)S(1)}, bf16[128,512]{1,0:T(8,128)(2,1)S(1)}, u32[]{:S(2)}, u32[]{:S(2)}) collective-permute-start(bf16[128,512]{1,0:T(8,128)(2,1)S(1)} %get-tuple-element.69), channel_id=1, source_target_pairs={{0,2},{1,3},{2,0},{3,1},{4,6},{5,7},{6,4},{7,5},{8,10},{9,11},{10,... | collective-permute-start | bytes 393224 | tf_op jit(solution)/shard_map/ppermute | solution.py:239
  139.5 11.1 %collective-permute-start.36 = (bf16[128,512]{1,0:T(8,128)(2,1)S(1)}, bf16[128,512]{1,0:T(8,128)(2,1)S(1)}, u32[]{:S(2)}, u32[]{:S(2)}) collective-permute-start(bf16[128,512]{1,0:T(8,128)(2,1)S(1)} %get-tuple-element.69), channel_id=1, source_target_pairs={{0,6},{1,7},{2,4},{3,5},{4,2},{5,3},{6,0},{7,1},{8,14},{9,15},{10,... | collective-permute-start | bytes 393224 | tf_op jit(solution)/shard_map/ppermute | solution.py:239
  150.9 8.4 %collective-permute-start.41 = (bf16[128,512]{1,0:T(8,128)(2,1)S(1)}, bf16[128,512]{1,0:T(8,128)(2,1)S(1)}, u32[]{:S(2)}, u32[]{:S(2)}) collective-permute-start(bf16[128,512]{1,0:T(8,128)(2,1)S(1)} %get-tuple-element.72), channel_id=1, source_target_pairs={{0,8},{1,9},{2,10},{3,11},{4,12},{5,13},{6,14},{7,15},{8,16},{9,17... | collective-permute-start | bytes 393224 | tf_op jit(solution)/shard_map/ppermute | solution.py:249
  150.9 8.4 %collective-permute-start.39 = (bf16[128,512]{1,0:T(8,128)(2,1)S(1)}, bf16[128,512]{1,0:T(8,128)(2,1)S(1)}, u32[]{:S(2)}, u32[]{:S(2)}) collective-permute-start(bf16[128,512]{1,0:T(8,128)(2,1)S(1)} %get-tuple-element.71), channel_id=1, source_target_pairs={{0,10},{1,11},{2,8},{3,9},{4,14},{5,15},{6,12},{7,13},{8,18},{9,19... | collective-permute-start | bytes 393224 | tf_op jit(solution)/shard_map/ppermute | solution.py:249
  161.6 10.4 %collective-permute-start.44 = (bf16[128,512]{1,0:T(8,128)(2,1)S(1)}, bf16[128,512]{1,0:T(8,128)(2,1)S(1)}, u32[]{:S(2)}, u32[]{:S(2)}) collective-permute-start(bf16[128,512]{1,0:T(8,128)(2,1)S(1)} %get-tuple-element.74.refs_0_), channel_id=1, source_target_pairs={{0,4},{1,5},{2,6},{3,7},{4,0},{5,1},{6,2},{7,3},{8,12},{9,13},{10,... | collective-permute-start | bytes 393224 | tf_op jit(solution)/shard_map/ppermute | solution.py:239
  164.0 7.9 %collective-permute-start.45 = (bf16[128,512]{1,0:T(8,128)(2,1)S(1)}, bf16[128,512]{1,0:T(8,128)(2,1)S(1)}, u32[]{:S(2)}, u32[]{:S(2)}) collective-permute-start(bf16[128,512]{1,0:T(8,128)(2,1)S(1)} %get-tuple-element.73), channel_id=1, source_target_pairs={{0,2},{1,3},{2,0},{3,1},{4,6},{5,7},{6,4},{7,5},{8,10},{9,11},{10,... | collective-permute-start | bytes 393224 | tf_op jit(solution)/shard_map/ppermute | solution.py:239
  164.1 11.0 %collective-permute-start.43 = (bf16[128,512]{1,0:T(8,128)(2,1)S(1)}, bf16[128,512]{1,0:T(8,128)(2,1)S(1)}, u32[]{:S(2)}, u32[]{:S(2)}) collective-permute-start(bf16[128,512]{1,0:T(8,128)(2,1)S(1)} %get-tuple-element.73), channel_id=1, source_target_pairs={{0,6},{1,7},{2,4},{3,5},{4,2},{5,3},{6,0},{7,1},{8,14},{9,15},{10,... | collective-permute-start | bytes 393224 | tf_op jit(solution)/shard_map/ppermute | solution.py:239
  (18 other events, 42.9 us)
